TPU v7x, 512 devices: a whole 4x8x8 slice. The times are simulated.
512 devices in a mesh: ctx: 32 (over y_lo, z), exp: 16 (over x, y_hi, core).
Axes of the slice: x: 4, y: 8 (y_hi: 2, y_lo: 4; y = y_hi * 4 + y_lo), z: 8, core: 2. Of those that a mesh axis runs over, the one named last changes fastest.
Arguments:
- queries: bfloat16 [2048, 4096], P('ctx', 'exp'), may hold values from -256 to 256
- keys: bfloat16 [2048, 1024], P('ctx'), may hold values from -6 to 6
- values: bfloat16 [2048, 1024], P('ctx'), may hold values from -6 to 6
- residual: bfloat16 [2048, 4096], P('ctx', 'exp'), may hold values from -20 to 20
- gain: bfloat16 [4096], P('exp'), may hold values from 0.5 to 2
- expert_ids: int32 [2048, 2], replicated, may hold values from 0 to 7, all different within a row; in each aligned block of 64 rows (0 to 63, 64 to 127, ...) at most 24 rows name the same one
- gate_weights: float32 [2048, 2], P('ctx'), may hold values from 0.2 to 1
- w_gate: bfloat16 [16, 4096, 4096], P('exp', None, 'ctx'), may hold values from -0.09375 to 0.09375
- w_up: bfloat16 [16, 4096, 4096], P('exp', None, 'ctx'), may hold values from -0.09375 to 0.09375
- w_down: bfloat16 [16, 4096, 4096], P('exp', None, 'ctx'), may hold values from -0.0625 to 0.0625
Outputs:
- mixed: bfloat16 [2048, 4096], P('ctx', 'exp')
Inputs may be any that keep to these rules, and one draw needn't show every extreme that they name: `expert_ids`: A token's 2 experts differ. In each aligned block of 64 tokens no expert is named by more than 24 tokens, a bound that some block reaches.
All inputs are finite; a program needn't handle non-finite values.
Results may differ from a plain program's by a relative error of at most 0.015.
Values may be sent and summed in bfloat16 or wider, within the bound.
No kernel may reach another device: no remote copies, remote signals or barrier semaphores. Data moves between devices by JAX's collectives and lax.ppermute only.
A program may use at most 64 MiB of HBM per device.

v0:
```python
import math

import jax
import jax.numpy as jnp
from jax import lax
from jax.sharding import PartitionSpec as P

D = 4096
HEADS = 32
KV_HEADS = 8
HEAD_DIM = 128
EXPERTS = 8
CAP = 24


epsilon = 1e-05
masked_score = -1e30


def slot_numbers(routing):
    flat = routing.reshape(-1)
    hits = (flat[:, None] == jnp.arange(EXPERTS, dtype=jnp.int32)[None, :]).astype(jnp.int32)
    before = jnp.cumsum(hits, axis=0) - hits
    return jnp.sum(before * hits, axis=1).reshape(routing.shape)


def placement_table(routing, weights):
    slots = slot_numbers(routing)
    expert_hit = (
        routing[:, :, None] == jnp.arange(EXPERTS, dtype=jnp.int32)[None, None, :]
    ).astype(jnp.float32)
    slot_hit = (slots[:, :, None] == jnp.arange(CAP, dtype=jnp.int32)[None, None, :]).astype(
        jnp.float32
    )
    return jnp.einsum(
        "ske,skc,sk->ecs", expert_hit, slot_hit, weights, precision=lax.Precision.HIGHEST
    )


def shards(queries, keys, values, residual, gain, expert_ids, gate_weights, w_gate, w_up, w_down):
    seq_rows = queries.shape[0]
    ctx_count = lax.axis_size("ctx")
    exp_count = lax.axis_size("exp")
    ctx_index = lax.axis_index("ctx")
    exp_index = lax.axis_index("exp")
    local_heads = queries.shape[1] // HEAD_DIM
    group = HEADS // KV_HEADS
    shared_heads = max(local_heads // group, 1)
    per_shared = local_heads // shared_heads
    first_shared = exp_index * local_heads // group
    key_part = lax.dynamic_slice_in_dim(keys, first_shared * HEAD_DIM, shared_heads * HEAD_DIM, 1)
    value_part = lax.dynamic_slice_in_dim(
        values, first_shared * HEAD_DIM, shared_heads * HEAD_DIM, 1
    )
    query_view = queries.reshape(seq_rows, shared_heads, per_shared, HEAD_DIM)
    positions = ctx_index * seq_rows + jnp.arange(seq_rows, dtype=jnp.int32)
    scale = 1.0 / math.sqrt(HEAD_DIM)
    running_max = jnp.full((shared_heads, per_shared, seq_rows), masked_score, jnp.float32)
    key_piece = lax.all_gather(key_part, "ctx", axis=0, tiled=True)
    value_piece = lax.all_gather(value_part, "ctx", axis=0, tiled=True)
    count = key_piece.shape[0]
    key_view = key_piece.reshape(count, shared_heads, HEAD_DIM)
    value_view = value_piece.reshape(count, shared_heads, HEAD_DIM)
    scores = (
        jnp.einsum("skgd,nkd->kgsn", query_view, key_view, preferred_element_type=jnp.float32)
        * scale
    )
    visible = positions[:, None] >= jnp.arange(count, dtype=jnp.int32)[None, :]
    scores = jnp.where(visible, scores, masked_score)
    new_max = jnp.maximum(running_max, jnp.max(scores, axis=-1))
    weights = jnp.where(visible, jnp.exp(scores - new_max[..., None]), 0.0)
    new_total = jnp.sum(weights, axis=-1)
    new_sum = jnp.einsum(
        "kgsn,nkd->kgsd",
        weights.astype(jnp.bfloat16),
        value_view,
        preferred_element_type=jnp.float32,
    )
    heads_out = new_sum / new_total[..., None]
    heads = (
        jnp.transpose(heads_out, (2, 0, 1, 3))
        .reshape(seq_rows, local_heads * HEAD_DIM)
        .astype(jnp.bfloat16)
    )
    stream = (residual.astype(jnp.float32) + heads.astype(jnp.float32)).astype(jnp.bfloat16)
    stream_wide = stream.astype(jnp.float32)
    square_total = lax.psum(jnp.sum(stream_wide * stream_wide, axis=1), "exp")
    mean_square = square_total / D
    normed = (
        stream_wide * lax.rsqrt(mean_square + epsilon)[:, None] * gain.astype(jnp.float32)[None, :]
    ).astype(jnp.bfloat16)
    width = normed.shape[1]
    held = w_gate.shape[0]
    split = exp_count * held // EXPERTS
    block_ids = lax.dynamic_slice_in_dim(expert_ids, ctx_index * seq_rows, seq_rows, 0)
    table = placement_table(block_ids, jnp.ones_like(gate_weights)).astype(jnp.bfloat16)
    outgoing = jnp.einsum("ecs,sd->ecd", table, normed, preferred_element_type=jnp.float32).astype(
        jnp.bfloat16
    )
    outgoing = jnp.repeat(outgoing, split, axis=0).reshape(exp_count, held, CAP, width)
    arrived = lax.all_to_all(outgoing, "exp", split_axis=0, concat_axis=3, tiled=True)
    piece = lax.all_gather(arrived[0], "ctx", axis=1, tiled=True)
    gate = jnp.einsum("end,edf->enf", piece, w_gate, preferred_element_type=jnp.float32)
    upper = jnp.einsum("end,edf->enf", piece, w_up, preferred_element_type=jnp.float32)
    activated = (jax.nn.silu(gate) * upper).astype(jnp.bfloat16)
    column_width = w_down.shape[2]
    expert_sums = jnp.einsum(
        "ern,enc->erc",
        lax.all_gather(activated, "ctx", axis=2, tiled=True),
        w_down,
        preferred_element_type=jnp.float32,
    )
    expert_out = expert_sums.astype(jnp.bfloat16).reshape(held, ctx_count, CAP, column_width)
    returned = lax.all_to_all(
        lax.all_to_all(expert_out, "ctx", split_axis=1, concat_axis=3, tiled=True),
        "exp",
        split_axis=3,
        concat_axis=0,
        tiled=True,
    )
    returned = returned[:, 0].astype(jnp.float32)
    weighted = jnp.repeat(placement_table(block_ids, gate_weights), split, axis=0)
    routed = jnp.einsum("ics,icd->sd", weighted, returned, precision=lax.Precision.HIGHEST)
    return (stream_wide + routed).astype(jnp.bfloat16)


def solution(mesh):
    return jax.shard_map(
        shards,
        mesh=mesh,
        in_specs=(
            P("ctx", "exp"),
            P("ctx", None),
            P("ctx", None),
            P("ctx", "exp"),
            P("exp"),
            P(),
            P("ctx", None),
            P("exp", None, "ctx"),
            P("exp", None, "ctx"),
            P("exp", None, "ctx"),
        ),
        out_specs=P("ctx", "exp"),
        check_vma=False,
    )
```

profile of v0, /device:TPU:1, one launch (start us, length us, event | category | flops | bytes accessed | tf_op | source)
XLA Modules:
  0.0 635.9 jit_solution(1990015575834860717)
XLA Ops:
  6.6 0.8 constant_dynamic-slice_fusion.2
  7.4 74.9 %all_gather.12 = bf16[2048,128]{1,0:T(8,128)(2,1)S(1)} all-gather(bf16[64,128]{1,0:T(8,128)(2,1)S(1)} %constant_dynamic-slice_fusion.2), channel_id=1, replica_groups=mesh['ctx'=32,'exp'=16] {'ctx'}, dimensions={0}, use_global_device_ids=true | all-gather | bytes 540672 | tf_op jit(solution)/shard_map/all_gather | solution.py:59
  82.3 0.1 iota_compare_fusion
  82.4 1.2 fusion.54
  83.6 0.7 constant_dynamic-slice_fusion.1
  84.3 62.1 %all_gather.13 = bf16[2048,128]{1,0:T(8,128)(2,1)S(1)} all-gather(bf16[64,128]{1,0:T(8,128)(2,1)S(1)} %constant_dynamic-slice_fusion.1), channel_id=1, replica_groups=mesh['ctx'=32,'exp'=16] {'ctx'}, dimensions={0}, use_global_device_ids=true | all-gather | bytes 540672 | tf_op jit(solution)/shard_map/all_gather | solution.py:60
  146.5 0.4 fusion.22
  146.9 0.4 fusion.18
  147.5 70.0 %psum.7 = f32[64]{0:T(128)S(1)} all-reduce(f32[64]{0:T(128)S(1)} %get-tuple-element.5), channel_id=1, replica_groups=mesh['ctx'=32,'exp'=16] {'exp'}, use_global_device_ids=true, to_apply=%region_5.6 | all-reduce | flops 64 | bytes 512 | tf_op jit(solution)/shard_map/psum | solution.py:87
  217.5 0.8 constant_dynamic-slice_fusion
  218.5 0.2 reduce_window_sum.12
  218.7 0.2 select_reduce_fusion
  219.0 0.4 fusion.12
  219.5 0.2 convolution_convert_fusion.2
  219.8 13.6 %all_to_all.48 = bf16[16,1,24,256]{3,2,1,0:T(8,128)(2,1)S(1)} all-to-all(bf16[16,1,24,256]{3,2,1,0:T(8,128)(2,1)S(1)} %bitcast.109), channel_id=1, replica_groups=mesh['ctx'=32,'exp'=16] {'exp'}, dimensions={0} | all-to-all | bytes 393216 | tf_op jit(solution)/shard_map/all_to_all | solution.py:101
  233.4 0.8 squeeze.6
  234.2 136.5 %all-gather.4.cloned.1.call-done = bf16[1,768,4096]{2,1,0:T(8,128)(2,1)} async-done(((bf16[1,24,4096]{2,1,0:T(8,128)(2,1)}), bf16[1,768,4096]{2,1,0:T(8,128)(2,1)}) %all-gather.4.cloned.1.call-update) | async-done | bytes 6291472 | tf_op jit(solution)/shard_map/all_gather | solution.py:102
  370.7 4.7 fusion.2
  375.5 2.5 fusion.9
  378.0 152.0 %all-gather.6.cloned.1.call-done = bf16[768,4096]{1,0:T(8,128)(2,1)} async-done(((bf16[768,128]{1,0:T(8,128)(2,1)}), bf16[768,4096]{1,0:T(8,128)(2,1)}) %all-gather.6.cloned.1.call-update) | async-done | bytes 6291472 | tf_op jit(solution)/shard_map/all_gather | solution.py:109
  530.0 4.6 convolution_convert_fusion
  534.5 16.3 %all_to_all.49 = bf16[1,32,24,128]{3,2,0,1:T(8,128)(2,1)S(1)} all-to-all(bf16[1,32,24,128]{3,2,0,1:T(8,128)(2,1)S(1)} %bitcast.112), channel_id=1, replica_groups=mesh['ctx'=32,'exp'=16] {'ctx'}, dimensions={1} | all-to-all | bytes 393216 | tf_op jit(solution)/shard_map/all_to_all | solution.py:115
  550.9 2.8 copy.35
  553.7 0.5 broadcast.43
  554.2 23.4 %reduce.2 = bf16[4096,24]{1,0:T(8,128)(2,1)} reduce(bf16[4096,1,1,24]{3,2,1,0:T(2,128)(2,1)S(1)} %bitcast.105, bf16[]{:T(256)} %broadcast.43), dimensions={1,2}, to_apply=%bitcast.91.reduce_sub_computation | reduce | bytes 393218
  577.6 3.3 reshape.102
  580.9 31.4 %all-to-all-start.2 = ((bf16[16,2,3072]{2,1,0:T(2,128)(2,1)}), bf16[16,2,3072]{2,1,0:T(2,128)(2,1)S(1)}, u32[]{:S(2)}, u32[]{:S(2)}) async-start(bf16[16,2,3072]{2,1,0:T(2,128)(2,1)} %reshape.102), calls=%async_computation.2 | async-start | bytes 393216 | tf_op jit(solution)/shard_map/all_to_all | solution.py:114
  612.4 0.6 convolution_bitcast_fusion
  613.2 9.8 %all-to-all-done.2 = bf16[16,2,3072]{2,1,0:T(2,128)(2,1)S(1)} async-done(((bf16[16,2,3072]{2,1,0:T(2,128)(2,1)}), bf16[16,2,3072]{2,1,0:T(2,128)(2,1)S(1)}, u32[]{:S(2)}, u32[]{:S(2)}) %all-to-all-start.2) | async-done | bytes 196640 | tf_op jit(solution)/shard_map/all_to_all | solution.py:114
  623.0 3.0 reshape.103
  625.9 2.1 copy.36
  628.1 1.0 fusion.15
  (34 shorter events, 1.1 us)
Async XLA Ops:
  6.5 364.2 %copy-start = (bf16[1,4096,128]{2,1,0:T(8,128)(2,1)S(1)}, bf16[1,4096,128]{2,1,0:T(8,128)(2,1)}, u32[]{:S(2)}) copy-start(bf16[1,4096,128]{2,1,0:T(8,128)(2,1)} %param.17) | copy-start | bytes 3145732
  6.5 140.8 %copy-start.1 = (bf16[64,256]{1,0:T(8,128)(2,1)S(1)}, bf16[64,256]{1,0:T(8,128)(2,1)}, u32[]{:S(2)}) copy-start(bf16[64,256]{1,0:T(8,128)(2,1)} %param.13) | copy-start | bytes 98308
  6.5 212.9 %copy-start.6 = (bf16[256]{0:T(256)(128)(2,1)S(1)}, bf16[256]{0:T(256)(128)(2,1)}, u32[]{:S(2)}) copy-start(bf16[256]{0:T(256)(128)(2,1)} %param.14) | copy-start | bytes 1540
  6.5 364.2 %all-gather.4.cloned.1.call-start = ((), (), s32[]{:S(2)}) async-start(), calls=%async_computation.3 | async-start | bytes 6488064 | tf_op jit(solution)/shard_map/all_gather | solution.py:102
  146.9 228.6 %copy-start.4 = (bf16[1,4096,128]{2,1,0:T(8,128)(2,1)S(1)}, bf16[1,4096,128]{2,1,0:T(8,128)(2,1)}, u32[]{:S(2)}) copy-start(bf16[1,4096,128]{2,1,0:T(8,128)(2,1)} %param.18) | copy-start | bytes 3145732
  234.2 295.8 %all-gather.6.cloned.1.call-start = ((), (), s32[]{:S(2)}) async-start(), calls=%async_computation.4 | async-start | bytes 6488064 | tf_op jit(solution)/shard_map/all_gather | solution.py:109
  370.7 4.7 copy-start.3
  375.4 154.5 %copy-start.5 = (bf16[1,4096,128]{2,1,0:T(8,128)(2,1)S(1)}, bf16[1,4096,128]{2,1,0:T(8,128)(2,1)}, u32[]{:S(2)}) copy-start(bf16[1,4096,128]{2,1,0:T(8,128)(2,1)} %param.19) | copy-start | bytes 3145732
  377.9 234.4 %copy-start.2 = (f32[64,2]{0,1:T(2,128)S(1)}, f32[64,2]{0,1:T(2,128)}, u32[]{:S(2)}) copy-start(f32[64,2]{0,1:T(2,128)} %param.16) | copy-start | bytes 1540
  580.9 42.1 %all-to-all-start.2 = ((bf16[16,2,3072]{2,1,0:T(2,128)(2,1)}), bf16[16,2,3072]{2,1,0:T(2,128)(2,1)S(1)}, u32[]{:S(2)}, u32[]{:S(2)}) async-start(bf16[16,2,3072]{2,1,0:T(2,128)(2,1)} %reshape.102), calls=%async_computation.2 | async-start | bytes 393216 | tf_op jit(solution)/shard_map/all_to_all | solution.py:114
Sparse Core Ops, SparseCore 0:
  234.3 136.3 all-gather.3
  378.1 151.8 all-gather.5
where the time goes:
time: 637 us; the launch traced here: 636 us
  waiting for transfers between devices  298 us (47%)
  blocking collectives  237 us (37%)
  starting transfers between devices  31.5 us (5%)
  other arithmetic  24.5 us (4%)
  matrix products  15.6 us (2%)
  local copies, waits for them, and re-layouts  15.5 us (2%)
  between operations  13.6 us (2%)
    all_gather x1, waiting for transfers between devices, shards(): lax.all_gather(activated, 'ctx', axis=2, tiled=True)  152 us
    all_gather x1, waiting for transfers between devices, shards(): piece = lax.all_gather(arrived[0], 'ctx', axis=1, tiled=True)  136 us
    all_gather x1, blocking collectives, shards(): key_piece = lax.all_gather(key_part, 'ctx', axis=0, tiled=True)  74.9 us
    psum x1, blocking collectives, shards(): square_total = lax.psum(jnp.sum(stream_wide * stream_wide, axis=1), 'exp')  70 us
    all_gather x1, blocking collectives, shards(): value_piece = lax.all_gather(value_part, 'ctx', axis=0, tiled=True)  62.1 us
    all_to_all x1, starting transfers between devices, shards(): lax.all_to_all(lax.all_to_all(expert_out, 'ctx', split_axis=1, concat_axi...  31.4 us
    unnamed x1, other arithmetic  23.4 us
    all_to_all x1, blocking collectives, shards(): lax.all_to_all(expert_out, 'ctx', split_axis=1, concat_axis=3, tiled=True)  16.3 us
  transfers between devices with their start and end apart: 3, of which 3 were waited for; matrix products, arithmetic and copies ran while one was open for 0% of the time, Pallas kernels for 0%

commit v1 on v0

v1 whole, which is shorter than its diff:
```python
import math

import jax
import jax.numpy as jnp
from jax import lax
from jax.experimental import pallas as pl
from jax.experimental.pallas import tpu as pltpu
from jax.sharding import Mesh, PartitionSpec as P

D = 4096
HEADS = 32
KV_HEADS = 8
HEAD_DIM = 128
EXPERTS = 8
CAP = 24
HALF = CAP // 2
PAD = 16

epsilon = 1e-05
masked_score = -1e30

CTX = ("yp", "ya", "z")
EXP = ("x", "h", "k")
SWAP = [(0, 1), (1, 0)]


def swap(value, axis):
    return lax.ppermute(value, axis, SWAP)


def slot_rows(routing):
    tokens, top = routing.shape
    flat = routing.reshape(-1)
    hits = (flat[:, None] == jnp.arange(EXPERTS, dtype=jnp.int32)[None, :]).astype(jnp.bfloat16)
    count = tokens * top
    order = jnp.arange(count, dtype=jnp.int32)
    earlier = (order[:, None] > order[None, :]).astype(jnp.bfloat16)
    before = jnp.dot(earlier, hits, preferred_element_type=jnp.float32)
    slots = jnp.sum(before * hits.astype(jnp.float32), axis=1).astype(jnp.int32)
    rows = flat * (2 * PAD) + jnp.where(slots >= HALF, slots - HALF + PAD, slots)
    return rows.reshape(tokens, top)


def attention(queries, keys, values, first):
    rows = queries.shape[0]
    heads = queries.shape[1] // HEAD_DIM
    query = jnp.transpose(queries.reshape(rows, heads, HEAD_DIM), (1, 0, 2)).reshape(
        heads * rows, HEAD_DIM
    )
    scores = lax.dot_general(
        query, keys, (((1,), (1,)), ((), ())), preferred_element_type=jnp.float32
    ) * (1.0 / math.sqrt(HEAD_DIM))
    count = keys.shape[0]
    positions = first + jnp.arange(heads * rows, dtype=jnp.int32) % rows
    visible = positions[:, None] >= jnp.arange(count, dtype=jnp.int32)[None, :]
    scores = jnp.where(visible, scores, masked_score)
    highest = jnp.max(scores, axis=1, keepdims=True)
    weights = jnp.where(visible, jnp.exp(scores - highest), 0.0)
    total = jnp.sum(weights, axis=1, keepdims=True)
    summed = jnp.dot(weights.astype(jnp.bfloat16), values, preferred_element_type=jnp.float32)
    out = (summed / total).reshape(heads, rows, HEAD_DIM)
    return jnp.transpose(out, (1, 0, 2)).reshape(rows, heads * HEAD_DIM).astype(jnp.bfloat16)


def gate_up_kernel(place, rows, *refs):
    gates, uppers, out, total = refs[0:4], refs[4:8], refs[8], refs[9]
    step = pl.program_id(0)

    @pl.when(step == 0)
    def _():
        total[...] = jnp.zeros_like(total)

    weights = jnp.concatenate([ref[...] for ref in gates + uppers], axis=1)
    total[...] += jnp.dot(rows[...], weights, preferred_element_type=jnp.float32)

    @pl.when(step == pl.num_programs(0) - 1)
    def _():
        width = total.shape[1] // 2
        gate = total[:, :width]
        upper = total[:, width:]
        hidden = (gate / (1.0 + jnp.exp(-gate)) * upper).astype(jnp.bfloat16)
        first = place[1] == 0
        unit = width // 4
        for part in range(2):
            mine = hidden[:, 2 * part * unit : (2 * part + 1) * unit]
            other = hidden[:, (2 * part + 1) * unit : (2 * part + 2) * unit]
            out[:, 2 * part * unit : (2 * part + 1) * unit] = jnp.where(first, mine, other)
            out[:, (2 * part + 1) * unit : (2 * part + 2) * unit] = jnp.where(first, other, mine)


def gate_up(place, rows, gates, uppers):
    count, depth = rows.shape
    unit = gates[0].shape[1]
    chunk = 512
    return pl.pallas_call(
        gate_up_kernel,
        out_shape=jax.ShapeDtypeStruct((count, 4 * unit), jnp.bfloat16),
        grid_spec=pltpu.PrefetchScalarGridSpec(
            num_scalar_prefetch=1,
            grid=(depth // chunk,),
            in_specs=[pl.BlockSpec((count, chunk), lambda i, place: (0, i))]
            + [pl.BlockSpec((chunk, unit), lambda i, place: (i, 0))] * 8,
            out_specs=pl.BlockSpec((count, 4 * unit), lambda i, place: (0, 0)),
            scratch_shapes=[pltpu.VMEM((count, 8 * unit), jnp.float32)],
        ),
        compiler_params=pltpu.CompilerParams(vmem_limit_bytes=32 * 1024 * 1024),
        cost_estimate=pl.CostEstimate(
            flops=2 * count * depth * 8 * unit,
            bytes_accessed=2 * depth * (count + 8 * unit),
            transcendentals=count * 4 * unit,
        ),
    )(place, rows, *gates, *uppers)


def down_kernel(place, mine, other, *refs):
    weights, out = refs[0:4], refs[4]
    first = place[0] == 0
    unit = mine.shape[1] // 4
    total = None
    for part in range(2):
        own = mine[:, 2 * part * unit : (2 * part + 2) * unit]
        far = other[:, 2 * part * unit : (2 * part + 2) * unit]
        hidden = jnp.concatenate([jnp.where(first, own, far), jnp.where(first, far, own)], axis=1)
        columns = jnp.concatenate([weights[2 * part][0], weights[2 * part + 1][0]], axis=1)
        product = jnp.dot(hidden, columns, preferred_element_type=jnp.float32)
        total = product if total is None else total + product
    total = total.astype(jnp.bfloat16)
    width = total.shape[1] // 2
    out[place[1]] = total[:, :width]
    out[1 - place[1]] = total[:, width:]


def down(place, mine, other, weights):
    count = mine.shape[0]
    groups, depth, unit = weights[0].shape
    return pl.pallas_call(
        down_kernel,
        out_shape=jax.ShapeDtypeStruct((2, count, groups * unit), jnp.bfloat16),
        grid_spec=pltpu.PrefetchScalarGridSpec(
            num_scalar_prefetch=1,
            grid=(groups,),
            in_specs=[pl.BlockSpec(mine.shape, lambda i, place: (0, 0))] * 2
            + [pl.BlockSpec((1, depth, unit), lambda i, place: (i, 0, 0))] * 4,
            out_specs=pl.BlockSpec((2, count, unit), lambda i, place: (0, 0, i)),
        ),
        compiler_params=pltpu.CompilerParams(vmem_limit_bytes=32 * 1024 * 1024),
        cost_estimate=pl.CostEstimate(
            flops=2 * count * 2 * depth * 2 * groups * unit,
            bytes_accessed=2 * (2 * count * mine.shape[1] + 4 * groups * depth * unit),
            transcendentals=0,
        ),
    )(place, mine, other, *weights)


def shards(queries, keys, values, residual, gain, expert_ids, gate_weights, w_gate, w_up, w_down):
    seq_rows = queries.shape[0]
    width = queries.shape[1]
    z_count = lax.axis_size("z")
    ctx_count = lax.axis_size(CTX)
    exp_count = lax.axis_size(EXP)
    ctx_index = lax.axis_index(CTX)
    core = lax.axis_index("k")
    place = jnp.stack([lax.axis_index("yp"), lax.axis_index("ya")]).astype(jnp.int32)

    head = (lax.axis_index("x") * 2 + lax.axis_index("h")) * HEAD_DIM
    key_part = lax.dynamic_slice_in_dim(keys, head, HEAD_DIM, 1)
    value_part = lax.dynamic_slice_in_dim(values, head, HEAD_DIM, 1)
    sent = jnp.where(core == 0, key_part, value_part)
    held = lax.all_to_all(
        jnp.broadcast_to(sent[None], (ctx_count, seq_rows, HEAD_DIM)), CTX, 0, 0, tiled=True
    ).reshape(ctx_count * seq_rows, HEAD_DIM)
    far = swap(held, "k")
    all_keys = jnp.where(core == 0, held, far)
    all_values = jnp.where(core == 0, far, held)

    def four(own):
        side = swap(own, "ya")
        return [own, side, swap(own, "k"), swap(side, "k")]

    gates = four(w_gate[0])
    uppers = four(w_up[0])
    unit = w_down.shape[2]
    cut = w_down[0].reshape(ctx_count // z_count, z_count, unit, unit)
    cut = jnp.transpose(cut, (1, 0, 2, 3)).reshape(z_count, ctx_count // z_count * unit, unit)
    downs = four(lax.all_to_all(cut, "z", 0, 0, tiled=True))

    heads = attention(queries, all_keys, all_values, ctx_index * seq_rows)
    stream = (residual.astype(jnp.float32) + heads.astype(jnp.float32)).astype(jnp.bfloat16)

    block_ids = lax.dynamic_slice_in_dim(expert_ids, ctx_index * seq_rows, seq_rows, 0)
    rows_of = slot_rows(block_ids)
    table_rows = EXPERTS * 2 * PAD
    row_id = jnp.arange(table_rows, dtype=jnp.int32)
    taken = (row_id[:, None] == rows_of[None, :, 0]) | (row_id[:, None] == rows_of[None, :, 1])
    gain_row = ((row_id % PAD) == HALF)[:, None]
    table = jnp.concatenate(
        [taken, gain_row, jnp.zeros((table_rows, 15), jnp.bool_)], axis=1
    ).astype(jnp.bfloat16)
    source = jnp.concatenate(
        [stream, gain[None, :], jnp.zeros((15, width), jnp.bfloat16)], axis=0
    )
    outgoing = jnp.dot(table, source, preferred_element_type=jnp.float32).astype(jnp.bfloat16)
    outgoing = jnp.broadcast_to(
        outgoing.reshape(1, exp_count, PAD, width), (2, exp_count, PAD, width)
    ).reshape(2 * exp_count, PAD, width)
    arrived = lax.all_to_all(outgoing, ("yp",) + EXP, 0, 0, tiled=True)
    arrived = arrived.reshape(2, exp_count, PAD, width).astype(jnp.float32)
    rows = arrived[:, :, :HALF]
    all_gain = arrived[0, :, HALF]
    mean_square = jnp.sum(rows * rows, axis=(1, 3), keepdims=True) / D
    normed = (rows * lax.rsqrt(mean_square + epsilon) * all_gain[None, :, None, :]).astype(
        jnp.bfloat16
    )
    piece = jnp.transpose(normed, (0, 2, 1, 3)).reshape(CAP, exp_count * width)

    all_rows = lax.all_gather(piece, "z", axis=0, tiled=True)
    hidden = gate_up(place, all_rows, gates, uppers)
    out = down(place, hidden, swap(hidden, "yp"), downs)

    half_columns = out.shape[2]
    back = out.reshape(2, z_count, 2, HALF, half_columns)
    back = jnp.transpose(back, (2, 1, 0, 3, 4)).reshape(2 * z_count, 2, HALF, half_columns)
    back = lax.all_to_all(back, ("yp", "z"), 0, 0, tiled=True)
    back = back.reshape(2, z_count, 2, HALF, half_columns).astype(jnp.float32)
    summed = jnp.sum(back, axis=1).astype(jnp.bfloat16)
    summed = summed.reshape(4, HALF, half_columns // width, width)
    summed = jnp.transpose(summed, (0, 2, 1, 3)).reshape(exp_count, HALF, width)
    summed = jnp.pad(summed, ((0, 0), (0, PAD - HALF), (0, 0)))
    returned = lax.all_to_all(summed, EXP, 0, 0, tiled=True).reshape(table_rows, width)
    mix = jnp.where(rows_of[:, 0:1] == row_id[None, :], gate_weights[:, 0:1], 0.0) + jnp.where(
        rows_of[:, 1:2] == row_id[None, :], gate_weights[:, 1:2], 0.0
    )
    routed = jnp.dot(mix, returned.astype(jnp.float32), precision=lax.Precision.HIGHEST)
    return (stream.astype(jnp.float32) + routed).astype(jnp.bfloat16)


def solution(mesh):
    split = Mesh(
        mesh.devices.reshape(2, 2, 8, 4, 2, 2), ("yp", "ya", "z", "x", "h", "k")
    )
    return jax.shard_map(
        shards,
        mesh=split,
        in_specs=(
            P(CTX, EXP),
            P(CTX, None),
            P(CTX, None),
            P(CTX, EXP),
            P(EXP),
            P(),
            P(CTX, None),
            P(EXP, None, CTX),
            P(EXP, None, CTX),
            P(EXP, None, CTX),
        ),
        out_specs=P(CTX, EXP),
        check_vma=False,
    )
```

time: 637 us -> 240 us (0.38)
  blocking collectives: 237 us -> 29.4 us
  waiting for transfers between devices: 298 us -> 92.8 us
  starting transfers between devices: 31.5 us -> 69 us
  other arithmetic: 24.5 us -> 2.29 us
  matrix products: 15.6 us -> 2.13 us
  Pallas kernels: 0 us -> 13.4 us
    all_gather x2 -> x1, waiting for transfers between devices: 288 us -> 0.01 us  [shards(): all_rows = lax.all_gather(piece, 'z', axis=0, tiled=True)]
    all_gather x2 -> x0, blocking collectives: 137 us -> none  [the longest x1 74.9 us: shards(): key_piece = lax.all_gather(key_part, 'ctx', axis=0, tiled=True)]
    psum x1 -> x0, blocking collectives: 70 us -> none  [shards(): square_total = lax.psum(jnp.sum(stream_wide * stream_wide, axis=1), 'exp')]
    all_to_all x1 -> x4, waiting for transfers between devices: 9.76 us -> 58.4 us  [the longest x1 23.2 us: shards(): downs = four(lax.all_to_all(cut, 'z', 0, 0, tiled=True))]
    ppermute x0 -> x11, starting transfers between devices: none -> 36.7 us  [swap(): return lax.ppermute(value, axis, SWAP)]
    ppermute x0 -> x11, waiting for transfers between devices: none -> 34.4 us  [swap(): return lax.ppermute(value, axis, SWAP)]
    unnamed x1 -> x0, other arithmetic: 23.4 us -> none
    dot_general x9 -> x5, matrix products: 15.6 us -> 2.13 us  [the longest x1 0.86 us: shards(): jnp.dot(mix, returned.astype(jnp.float32), precision=lax.Precision.HIGHEST)]
  transfers between devices with their start and end apart: 3 -> 16, of which waited for: 3 -> 8; matrix products, arithmetic and copies ran while one was open for 0% -> 1% of each run, Pallas kernels for 0% -> 3%
where the time goes in v1:
time: 240 us; the launch traced here: 238 us
  waiting for transfers between devices  92.8 us (39%)
  starting transfers between devices  69 us (29%)
  blocking collectives  29.4 us (12%)
  local copies, waits for them, and re-layouts  15.7 us (7%)
  between operations  13.8 us (6%)
  Pallas kernels  13.4 us (6%)
    ppermute x11, starting transfers between devices, swap(): return lax.ppermute(value, axis, SWAP)  36.7 us
    ppermute x11, waiting for transfers between devices, swap(): return lax.ppermute(value, axis, SWAP)  34.4 us
    all_to_all x1, blocking collectives, shards(): back = lax.all_to_all(back, ('yp', 'z'), 0, 0, tiled=True)  29.4 us
    all_to_all x1, waiting for transfers between devices, shards(): downs = four(lax.all_to_all(cut, 'z', 0, 0, tiled=True))  23.2 us
    all_to_all x1, starting transfers between devices, shards(): lax.all_to_all(jnp.broadcast_to(sent[None], (ctx_count, seq_rows, HEAD_DI...  14.3 us
    all_to_all x1, waiting for transfers between devices, shards(): lax.all_to_all(jnp.broadcast_to(sent[None], (ctx_count, seq_rows, HEAD_DI...  14 us
    all_to_all x1, waiting for transfers between devices, shards(): arrived = lax.all_to_all(outgoing, ('yp',) + EXP, 0, 0, tiled=True)  11.1 us
    all_to_all x1, waiting for transfers between devices, shards(): lax.all_to_all(summed, EXP, 0, 0, tiled=True).reshape(table_rows, width)  10 us
  transfers between devices with their start and end apart: 16, of which 8 were waited for; matrix products, arithmetic and copies ran while one was open for 1% of the time, Pallas kernels for 3%

profile of v1, /device:TPU:1, one launch (start us, length us, event | category | flops | bytes accessed | tf_op | source)
XLA Modules:
  0.0 238.4 jit_solution(5690494913489169794)
XLA Ops:
  8.2 14.3 %all-to-all-start = ((bf16[32,64,128]{2,1,0:T(8,128)(2,1)}), bf16[32,64,128]{2,1,0:T(8,128)(2,1)S(1)}, u32[]{:S(2)}, u32[]{:S(2)}) async-start(bf16[32,64,128]{2,1,0:T(8,128)(2,1)} %broadcast_in_dim.64), calls=%async_computation | async-start | bytes 1048576 | tf_op jit(solution)/shard_map/all_to_all | solution.py:169
  23.5 14.0 %all-to-all-done = bf16[32,64,128]{2,1,0:T(8,128)(2,1)S(1)} async-done(((bf16[32,64,128]{2,1,0:T(8,128)(2,1)}), bf16[32,64,128]{2,1,0:T(8,128)(2,1)S(1)}, u32[]{:S(2)}, u32[]{:S(2)}) %all-to-all-start) | async-done | bytes 524320 | tf_op jit(solution)/shard_map/all_to_all | solution.py:169
  37.4 4.8 %collective-permute-start = (bf16[2048,128]{1,0:T(8,128)(2,1)S(1)}, bf16[2048,128]{1,0:T(8,128)(2,1)S(1)}, u32[]{:S(2)}, u32[]{:S(2)}) collective-permute-start(bf16[2048,128]{1,0:T(8,128)(2,1)S(1)} %bitcast.69), channel_id=1, source_target_pairs={{0,1},{1,0},{2,3},{3,2},{4,5},{5,4},{6,7},{7,6},{8,9},{9,8},{10,11... | collective-permute-start | bytes 1572872 | tf_op jit(solution)/shard_map/ppermute | solution.py:28
  42.4 1.3 collective-permute-done
  46.2 7.4 %all-to-all-start.1 = ((bf16[32,16,256]{2,1,0:T(8,128)(2,1)}), bf16[32,16,256]{2,1,0:T(8,128)(2,1)S(1)}, u32[]{:S(2)}, u32[]{:S(2)}) async-start(bf16[32,16,256]{2,1,0:T(8,128)(2,1)} %bitcast.11), calls=%async_computation.1 | async-start | bytes 524288 | tf_op jit(solution)/shard_map/all_to_all | solution.py:206
  53.6 1.1 copy.43
  54.7 11.1 %all-to-all-done.1 = bf16[32,16,256]{2,1,0:T(8,128)(2,1)S(1)} async-done(((bf16[32,16,256]{2,1,0:T(8,128)(2,1)}), bf16[32,16,256]{2,1,0:T(8,128)(2,1)S(1)}, u32[]{:S(2)}, u32[]{:S(2)}) %all-to-all-start.1) | async-done | bytes 262176 | tf_op jit(solution)/shard_map/all_to_all | solution.py:206
  65.9 3.9 %all-to-all-start.2 = ((bf16[8,512,128]{2,1,0:T(8,128)(2,1)}), bf16[8,512,128]{2,1,0:T(8,128)(2,1)S(1)}, u32[]{:S(2)}, u32[]{:S(2)}) async-start(bf16[8,512,128]{2,1,0:T(8,128)(2,1)} %bitcast.19), calls=%async_computation.2 | async-start | bytes 2097152 | tf_op jit(solution)/shard_map/all_to_all | solution.py:185
  71.1 3.8 %collective-permute-start.1 = (bf16[4096,128]{1,0:T(8,128)(2,1)S(1)}, bf16[4096,128]{1,0:T(8,128)(2,1)}, u32[]{:S(2)}, u32[]{:S(2)}) collective-permute-start(bf16[4096,128]{1,0:T(8,128)(2,1)S(1)} %bitcast.57), channel_id=1, source_target_pairs={{0,128},{128,0},{1,129},{129,1},{2,130},{130,2},{3,131},{131,3},{4... | collective-permute-start | bytes 3145736 | tf_op jit(solution)/shard_map/ppermute | solution.py:28
  74.9 1.9 collective-permute-start.4
  76.9 3.3 %collective-permute-start.2 = (bf16[4096,128]{1,0:T(8,128)(2,1)S(1)}, bf16[4096,128]{1,0:T(8,128)(2,1)}, u32[]{:S(2)}, u32[]{:S(2)}) collective-permute-start(bf16[4096,128]{1,0:T(8,128)(2,1)S(1)} %bitcast.58), channel_id=1, source_target_pairs={{0,1},{1,0},{2,3},{3,2},{4,5},{5,4},{6,7},{7,6},{8,9},{9,8},{10,11... | collective-permute-start | bytes 3145736 | tf_op jit(solution)/shard_map/ppermute | solution.py:28
  80.2 23.2 %all-to-all-done.2.refs_0_ = bf16[8,512,128]{2,1,0:T(8,128)(2,1)S(1)} async-done(((bf16[8,512,128]{2,1,0:T(8,128)(2,1)}), bf16[8,512,128]{2,1,0:T(8,128)(2,1)S(1)}, u32[]{:S(2)}, u32[]{:S(2)}) %all-to-all-start.2) | async-done | bytes 1048608 | tf_op jit(solution)/shard_map/all_to_all | solution.py:185
  103.4 3.9 %collective-permute-start.8 = (bf16[8,512,128]{2,1,0:T(8,128)(2,1)S(1)}, bf16[8,512,128]{2,1,0:T(8,128)(2,1)}, u32[]{:S(2)}, u32[]{:S(2)}) collective-permute-start(bf16[8,512,128]{2,1,0:T(8,128)(2,1)S(1)} %all-to-all-done.2.refs_0_), channel_id=1, source_target_pairs={{0,128},{128,0},{1,129},{129,1},{2,130},{130,2},{3,131},{131,3},{4... | collective-permute-start | bytes 3145736 | tf_op jit(solution)/shard_map/ppermute | solution.py:28
  107.3 3.2 %collective-permute-start.5 = (bf16[4096,128]{1,0:T(8,128)(2,1)S(1)}, bf16[4096,128]{1,0:T(8,128)(2,1)S(1)}, u32[]{:S(2)}, u32[]{:S(2)}) collective-permute-start(bf16[4096,128]{1,0:T(8,128)(2,1)S(1)} %bitcast.61), channel_id=1, source_target_pairs={{0,1},{1,0},{2,3},{3,2},{4,5},{5,4},{6,7},{7,6},{8,9},{9,8},{10,11... | collective-permute-start | bytes 3145736 | tf_op jit(solution)/shard_map/ppermute | solution.py:28
  110.5 1.9 collective-permute-start.3
  112.5 7.4 %collective-permute-done.4.refs_5_ = bf16[4096,128]{1,0:T(8,128)(2,1)} collective-permute-done((bf16[4096,128]{1,0:T(8,128)(2,1)S(1)}, bf16[4096,128]{1,0:T(8,128)(2,1)}, u32[]{:S(2)}, u32[]{:S(2)}) %collective-permute-start.4) | collective-permute-done | bytes 1048608 | tf_op jit(solution)/shard_map/ppermute | solution.py:28
  119.9 5.0 %collective-permute-start.6 = (bf16[4096,128]{1,0:T(8,128)(2,1)}, bf16[4096,128]{1,0:T(8,128)(2,1)S(1)}, u32[]{:S(2)}, u32[]{:S(2)}) collective-permute-start(bf16[4096,128]{1,0:T(8,128)(2,1)} %collective-permute-done.4.refs_5_), channel_id=1, source_target_pairs={{0,1},{1,0},{2,3},{3,2},{4,5},{5,4},{6,7},{7,6},{8,9},{9,8},{10,11... | collective-permute-start | bytes 3145736 | tf_op jit(solution)/shard_map/ppermute | solution.py:28
  124.8 1.9 collective-permute-start.9
  126.8 15.6 %collective-permute-done.8.refs_1_ = bf16[8,512,128]{2,1,0:T(8,128)(2,1)} collective-permute-done((bf16[8,512,128]{2,1,0:T(8,128)(2,1)S(1)}, bf16[8,512,128]{2,1,0:T(8,128)(2,1)}, u32[]{:S(2)}, u32[]{:S(2)}) %collective-permute-start.8) | collective-permute-done | bytes 1048608 | tf_op jit(solution)/shard_map/ppermute | solution.py:28
  142.3 3.6 %collective-permute-start.10 = (bf16[8,512,128]{2,1,0:T(8,128)(2,1)}, bf16[8,512,128]{2,1,0:T(8,128)(2,1)}, u32[]{:S(2)}, u32[]{:S(2)}) collective-permute-start(bf16[8,512,128]{2,1,0:T(8,128)(2,1)} %collective-permute-done.8.refs_1_), channel_id=1, source_target_pairs={{0,1},{1,0},{2,3},{3,2},{4,5},{5,4},{6,7},{7,6},{8,9},{9,8},{10,11... | collective-permute-start | bytes 3145736 | tf_op jit(solution)/shard_map/ppermute | solution.py:28
  147.0 1.0 copy-done.6
  149.0 1.4 copy-done.1
  150.4 1.2 copy-done.5
  151.7 1.2 copy-done.7
  152.9 1.2 copy-done.9
  154.1 7.0 %shard_map.100.mine = bf16[192,512]{1,0:T(8,128)(2,1)S(1)} custom-call(s32[2]{0:T(128)S(1)} %pad_add_fusion.place, bf16[192,4096]{1,0:T(8,128)(2,1)S(1)} %copy-done.1, bf16[4096,128]{1,0:T(8,128)(2,1)S(1)} %bitcast.59, bf16[4096,128]{1,0:T(8,128)(2,1)} %collective-permute-done.1.refs_1_, bf16[4096,128]{1,0:T(8,128)(2,1)} %collective-permute-done.2.refs_2_, ...), custom_call_target="tpu_custom_call" | custom-call | flops 1610612736 | bytes 9961472 | tf_op jit(solution)/shard_map/pallas_call | solution.py:95
  161.1 3.4 %collective-permute-start.7 = (bf16[192,512]{1,0:T(8,128)(2,1)S(1)}, bf16[192,512]{1,0:T(8,128)(2,1)S(1)}, u32[]{:S(2)}, u32[]{:S(2)}) collective-permute-start(bf16[192,512]{1,0:T(8,128)(2,1)S(1)} %shard_map.100.mine), channel_id=1, source_target_pairs={{0,256},{256,0},{1,257},{257,1},{2,258},{258,2},{3,259},{259,3},{4... | collective-permute-start | bytes 589832 | tf_op jit(solution)/shard_map/ppermute | solution.py:28
  164.5 10.1 %collective-permute-done.7.other = bf16[192,512]{1,0:T(8,128)(2,1)S(1)} collective-permute-done((bf16[192,512]{1,0:T(8,128)(2,1)S(1)}, bf16[192,512]{1,0:T(8,128)(2,1)S(1)}, u32[]{:S(2)}, u32[]{:S(2)}) %collective-permute-start.7) | collective-permute-done | bytes 196640 | tf_op jit(solution)/shard_map/ppermute | solution.py:28
  174.6 6.3 %shard_map.101 = bf16[2,192,1024]{2,1,0:T(8,128)(2,1)S(1)} custom-call(s32[2]{0:T(128)S(1)} %pad_add_fusion.place, bf16[192,512]{1,0:T(8,128)(2,1)S(1)} %shard_map.100.mine, bf16[192,512]{1,0:T(8,128)(2,1)S(1)} %collective-permute-done.7.other, bf16[8,512,128]{2,1,0:T(8,128)(2,1)S(1)} %all-to-all-done.2.refs_0_, ...), custom_call_target="tpu_custom_call" | custom-call | flops 805306368 | bytes 4587520 | tf_op jit(solution)/shard_map/pallas_call | solution.py:136
  183.1 29.4 %all_to_all.25 = bf16[16,2,12,1024]{3,1,2,0:T(2,128)(2,1)S(1)} all-to-all(bf16[16,2,12,1024]{3,1,2,0:T(2,128)(2,1)S(1)} %copy.46), channel_id=1, replica_groups=mesh['yp'=2,'ya'=2,'z'=8,'x'=4,'h'=2,'k'=2] {'yp','z'}, dimensions={0} | all-to-all | bytes 1572864 | tf_op jit(solution)/shard_map/all_to_all | solution.py:223
  214.1 6.6 %all-to-all-start.4 = ((bf16[16,16,256]{2,1,0:T(8,128)(2,1)}), bf16[16,16,256]{2,1,0:T(8,128)(2,1)S(1)}, u32[]{:S(2)}, u32[]{:S(2)}) async-start(bf16[16,16,256]{2,1,0:T(8,128)(2,1)} %pad.4.clone), calls=%async_computation.4 | async-start | bytes 262144 | tf_op jit(solution)/shard_map/all_to_all | solution.py:229
  220.7 10.0 %all-to-all-done.4 = bf16[16,16,256]{2,1,0:T(8,128)(2,1)S(1)} async-done(((bf16[16,16,256]{2,1,0:T(8,128)(2,1)}), bf16[16,16,256]{2,1,0:T(8,128)(2,1)S(1)}, u32[]{:S(2)}, u32[]{:S(2)}) %all-to-all-start.4) | async-done | bytes 131104 | tf_op jit(solution)/shard_map/all_to_all | solution.py:229
  (80 shorter events, 12.9 us)
Async XLA Ops:
  6.5 16.1 %copy-start = (s32[2048,2]{0,1:T(2,128)S(1)}, s32[2048,2]{0,1:T(2,128)}, u32[]{:S(2)}) copy-start(s32[2048,2]{0,1:T(2,128)} %param.15) | copy-start | bytes 49156
  6.5 16.0 %copy-start.12 = (bf16[64,256]{1,0:T(8,128)(2,1)S(1)}, bf16[64,256]{1,0:T(8,128)(2,1)}, u32[]{:S(2)}) copy-start(bf16[64,256]{1,0:T(8,128)(2,1)} %param.10) | copy-start | bytes 98308
  6.5 16.7 %copy-start.14 = (bf16[256]{0:T(256)(128)(2,1)S(1)}, bf16[256]{0:T(256)(128)(2,1)}, u32[]{:S(2)}) copy-start(bf16[256]{0:T(256)(128)(2,1)} %param.14) | copy-start | bytes 1540
  8.2 29.2 %all-to-all-start = ((bf16[32,64,128]{2,1,0:T(8,128)(2,1)}), bf16[32,64,128]{2,1,0:T(8,128)(2,1)S(1)}, u32[]{:S(2)}, u32[]{:S(2)}) async-start(bf16[32,64,128]{2,1,0:T(8,128)(2,1)} %broadcast_in_dim.64), calls=%async_computation | async-start | bytes 1048576 | tf_op jit(solution)/shard_map/all_to_all | solution.py:169
  37.4 6.3 %collective-permute-start = (bf16[2048,128]{1,0:T(8,128)(2,1)S(1)}, bf16[2048,128]{1,0:T(8,128)(2,1)S(1)}, u32[]{:S(2)}, u32[]{:S(2)}) collective-permute-start(bf16[2048,128]{1,0:T(8,128)(2,1)S(1)} %bitcast.69), channel_id=1, source_target_pairs={{0,1},{1,0},{2,3},{3,2},{4,5},{5,4},{6,7},{7,6},{8,9},{9,8},{10,11... | collective-permute-start | bytes 1572872 | tf_op jit(solution)/shard_map/ppermute | solution.py:28
  44.4 0.8 copy-start.11
  44.5 9.1 %copy-start.10 = (bf16[1,4096,128]{2,1,0:T(8,128)(2,1)S(1)}, bf16[1,4096,128]{2,1,0:T(8,128)(2,1)}, u32[]{:S(2)}) copy-start(bf16[1,4096,128]{2,1,0:T(8,128)(2,1)} %param.19) | copy-start | bytes 3145732
  46.2 19.7 %all-to-all-start.1 = ((bf16[32,16,256]{2,1,0:T(8,128)(2,1)}), bf16[32,16,256]{2,1,0:T(8,128)(2,1)S(1)}, u32[]{:S(2)}, u32[]{:S(2)}) async-start(bf16[32,16,256]{2,1,0:T(8,128)(2,1)} %bitcast.11), calls=%async_computation.1 | async-start | bytes 524288 | tf_op jit(solution)/shard_map/all_to_all | solution.py:206
  65.9 37.6 %all-to-all-start.2 = ((bf16[8,512,128]{2,1,0:T(8,128)(2,1)}), bf16[8,512,128]{2,1,0:T(8,128)(2,1)S(1)}, u32[]{:S(2)}, u32[]{:S(2)}) async-start(bf16[8,512,128]{2,1,0:T(8,128)(2,1)} %bitcast.19), calls=%async_computation.2 | async-start | bytes 2097152 | tf_op jit(solution)/shard_map/all_to_all | solution.py:185
  69.8 1.3 copy-start.2
  69.8 5.1 %copy-start.3 = (bf16[1,4096,128]{2,1,0:T(8,128)(2,1)S(1)}, bf16[1,4096,128]{2,1,0:T(8,128)(2,1)}, u32[]{:S(2)}) copy-start(bf16[1,4096,128]{2,1,0:T(8,128)(2,1)} %param.18) | copy-start | bytes 3145732
  69.8 79.2 %all-gather.2.cloned.1.call-start = ((), (), s32[]{:S(2)}) async-start(), calls=%async_computation.5 | async-start | bytes 1769472 | tf_op jit(solution)/shard_map/all_gather | solution.py:216
  71.1 39.4 %collective-permute-start.1 = (bf16[4096,128]{1,0:T(8,128)(2,1)S(1)}, bf16[4096,128]{1,0:T(8,128)(2,1)}, u32[]{:S(2)}, u32[]{:S(2)}) collective-permute-start(bf16[4096,128]{1,0:T(8,128)(2,1)S(1)} %bitcast.57), channel_id=1, source_target_pairs={{0,128},{128,0},{1,129},{129,1},{2,130},{130,2},{3,131},{131,3},{4... | collective-permute-start | bytes 3145736 | tf_op jit(solution)/shard_map/ppermute | solution.py:28
  74.9 44.9 %collective-permute-start.4 = (bf16[4096,128]{1,0:T(8,128)(2,1)S(1)}, bf16[4096,128]{1,0:T(8,128)(2,1)}, u32[]{:S(2)}, u32[]{:S(2)}) collective-permute-start(bf16[4096,128]{1,0:T(8,128)(2,1)S(1)} %bitcast.60), channel_id=1, source_target_pairs={{0,128},{128,0},{1,129},{129,1},{2,130},{130,2},{3,131},{131,3},{4... | collective-permute-start | bytes 3145736 | tf_op jit(solution)/shard_map/ppermute | solution.py:28
  76.9 48.0 %collective-permute-start.2 = (bf16[4096,128]{1,0:T(8,128)(2,1)S(1)}, bf16[4096,128]{1,0:T(8,128)(2,1)}, u32[]{:S(2)}, u32[]{:S(2)}) collective-permute-start(bf16[4096,128]{1,0:T(8,128)(2,1)S(1)} %bitcast.58), channel_id=1, source_target_pairs={{0,1},{1,0},{2,3},{3,2},{4,5},{5,4},{6,7},{7,6},{8,9},{9,8},{10,11... | collective-permute-start | bytes 3145736 | tf_op jit(solution)/shard_map/ppermute | solution.py:28
  103.4 38.9 %collective-permute-start.8 = (bf16[8,512,128]{2,1,0:T(8,128)(2,1)S(1)}, bf16[8,512,128]{2,1,0:T(8,128)(2,1)}, u32[]{:S(2)}, u32[]{:S(2)}) collective-permute-start(bf16[8,512,128]{2,1,0:T(8,128)(2,1)S(1)} %all-to-all-done.2.refs_0_), channel_id=1, source_target_pairs={{0,128},{128,0},{1,129},{129,1},{2,130},{130,2},{3,131},{131,3},{4... | collective-permute-start | bytes 3145736 | tf_op jit(solution)/shard_map/ppermute | solution.py:28
  107.3 38.8 %collective-permute-start.5 = (bf16[4096,128]{1,0:T(8,128)(2,1)S(1)}, bf16[4096,128]{1,0:T(8,128)(2,1)S(1)}, u32[]{:S(2)}, u32[]{:S(2)}) collective-permute-start(bf16[4096,128]{1,0:T(8,128)(2,1)S(1)} %bitcast.61), channel_id=1, source_target_pairs={{0,1},{1,0},{2,3},{3,2},{4,5},{5,4},{6,7},{7,6},{8,9},{9,8},{10,11... | collective-permute-start | bytes 3145736 | tf_op jit(solution)/shard_map/ppermute | solution.py:28
  110.5 36.5 %collective-permute-start.3 = (bf16[4096,128]{1,0:T(8,128)(2,1)}, bf16[4096,128]{1,0:T(8,128)(2,1)S(1)}, u32[]{:S(2)}, u32[]{:S(2)}) collective-permute-start(bf16[4096,128]{1,0:T(8,128)(2,1)} %collective-permute-done.1.refs_1_), channel_id=1, source_target_pairs={{0,1},{1,0},{2,3},{3,2},{4,5},{5,4},{6,7},{7,6},{8,9},{9,8},{10,11... | collective-permute-start | bytes 3145736 | tf_op jit(solution)/shard_map/ppermute | solution.py:28
  119.9 28.2 %collective-permute-start.6 = (bf16[4096,128]{1,0:T(8,128)(2,1)}, bf16[4096,128]{1,0:T(8,128)(2,1)S(1)}, u32[]{:S(2)}, u32[]{:S(2)}) collective-permute-start(bf16[4096,128]{1,0:T(8,128)(2,1)} %collective-permute-done.4.refs_5_), channel_id=1, source_target_pairs={{0,1},{1,0},{2,3},{3,2},{4,5},{5,4},{6,7},{7,6},{8,9},{9,8},{10,11... | collective-permute-start | bytes 3145736 | tf_op jit(solution)/shard_map/ppermute | solution.py:28
  124.8 39.6 %collective-permute-start.9 = (bf16[8,512,128]{2,1,0:T(8,128)(2,1)S(1)}, bf16[8,512,128]{2,1,0:T(8,128)(2,1)}, u32[]{:S(2)}, u32[]{:S(2)}) collective-permute-start(bf16[8,512,128]{2,1,0:T(8,128)(2,1)S(1)} %all-to-all-done.2.refs_0_), channel_id=1, source_target_pairs={{0,1},{1,0},{2,3},{3,2},{4,5},{5,4},{6,7},{7,6},{8,9},{9,8},{10,11... | collective-permute-start | bytes 3145736 | tf_op jit(solution)/shard_map/ppermute | solution.py:28
  142.3 22.2 %collective-permute-start.10 = (bf16[8,512,128]{2,1,0:T(8,128)(2,1)}, bf16[8,512,128]{2,1,0:T(8,128)(2,1)}, u32[]{:S(2)}, u32[]{:S(2)}) collective-permute-start(bf16[8,512,128]{2,1,0:T(8,128)(2,1)} %collective-permute-done.8.refs_1_), channel_id=1, source_target_pairs={{0,1},{1,0},{2,3},{3,2},{4,5},{5,4},{6,7},{7,6},{8,9},{9,8},{10,11... | collective-permute-start | bytes 3145736 | tf_op jit(solution)/shard_map/ppermute | solution.py:28
  146.1 1.0 copy-start.4
  147.0 1.0 copy-start.6
  148.1 1.0 copy-start.8
  149.0 1.4 copy-start.1
  150.4 1.2 copy-start.5
  151.7 1.2 copy-start.7
  152.9 1.2 copy-start.9
  161.1 13.5 %collective-permute-start.7 = (bf16[192,512]{1,0:T(8,128)(2,1)S(1)}, bf16[192,512]{1,0:T(8,128)(2,1)S(1)}, u32[]{:S(2)}, u32[]{:S(2)}) collective-permute-start(bf16[192,512]{1,0:T(8,128)(2,1)S(1)} %shard_map.100.mine), channel_id=1, source_target_pairs={{0,256},{256,0},{1,257},{257,1},{2,258},{258,2},{3,259},{259,3},{4... | collective-permute-start | bytes 589832 | tf_op jit(solution)/shard_map/ppermute | solution.py:28
  183.1 37.6 %copy-start.13 = (f32[64,2]{0,1:T(2,128)S(1)}, f32[64,2]{0,1:T(2,128)}, u32[]{:S(2)}) copy-start(f32[64,2]{0,1:T(2,128)} %param.16) | copy-start | bytes 1540
  214.1 16.7 %all-to-all-start.4 = ((bf16[16,16,256]{2,1,0:T(8,128)(2,1)}), bf16[16,16,256]{2,1,0:T(8,128)(2,1)S(1)}, u32[]{:S(2)}, u32[]{:S(2)}) async-start(bf16[16,16,256]{2,1,0:T(8,128)(2,1)} %pad.4.clone), calls=%async_computation.4 | async-start | bytes 262144 | tf_op jit(solution)/shard_map/all_to_all | solution.py:229
Sparse Core Ops, SparseCore 0:
  72.7 42.7 all-gather.1

commit v2 on v1

--- a/solution.py
+++ b/solution.py
@@ -62,36 +62,41 @@
     return jnp.transpose(out, (1, 0, 2)).reshape(rows, heads * HEAD_DIM).astype(jnp.bfloat16)
 
 
-def gate_up_kernel(place, rows, *refs):
-    gates, uppers, out, total = refs[0:4], refs[4:8], refs[8], refs[9]
+def gate_up_kernel(place, rows, gate_own, gate_far, *refs):
+    uppers, out, total = refs[0:4], refs[4], refs[5]
     step = pl.program_id(0)
+    columns = [gate_own[0], gate_own[1], gate_far[0], gate_far[1]] + [ref[...] for ref in uppers]
+    product = jnp.dot(
+        rows[...], jnp.concatenate(columns, axis=1), preferred_element_type=jnp.float32
+    )
 
     @pl.when(step == 0)
     def _():
-        total[...] = jnp.zeros_like(total)
-
-    weights = jnp.concatenate([ref[...] for ref in gates + uppers], axis=1)
-    total[...] += jnp.dot(rows[...], weights, preferred_element_type=jnp.float32)
+        total[...] = product
+
+    @pl.when(step != 0)
+    def _():
+        total[...] += product
 
     @pl.when(step == pl.num_programs(0) - 1)
     def _():
-        width = total.shape[1] // 2
-        gate = total[:, :width]
-        upper = total[:, width:]
-        hidden = (gate / (1.0 + jnp.exp(-gate)) * upper).astype(jnp.bfloat16)
+        unit = gate_own.shape[2]
         first = place[1] == 0
-        unit = width // 4
         for part in range(2):
-            mine = hidden[:, 2 * part * unit : (2 * part + 1) * unit]
-            other = hidden[:, (2 * part + 1) * unit : (2 * part + 2) * unit]
-            out[:, 2 * part * unit : (2 * part + 1) * unit] = jnp.where(first, mine, other)
-            out[:, (2 * part + 1) * unit : (2 * part + 2) * unit] = jnp.where(first, other, mine)
+            mine = total[:, (4 + 2 * part) * unit : (5 + 2 * part) * unit]
+            side = total[:, (5 + 2 * part) * unit : (6 + 2 * part) * unit]
+            for half in range(2):
+                at = 2 * part + half
+                gate = total[:, at * unit : (at + 1) * unit]
+                upper = jnp.where(first, mine, side) if half == 0 else jnp.where(first, side, mine)
+                hidden = gate / (1.0 + jnp.exp(-gate)) * upper
+                out[:, at * unit : (at + 1) * unit] = hidden.astype(jnp.bfloat16)
 
 
 def gate_up(place, rows, gates, uppers):
     count, depth = rows.shape
-    unit = gates[0].shape[1]
-    chunk = 512
+    unit = uppers[0].shape[1]
+    chunk = 1024
     return pl.pallas_call(
         gate_up_kernel,
         out_shape=jax.ShapeDtypeStruct((count, 4 * unit), jnp.bfloat16),
@@ -99,7 +104,8 @@
             num_scalar_prefetch=1,
             grid=(depth // chunk,),
             in_specs=[pl.BlockSpec((count, chunk), lambda i, place: (0, i))]
-            + [pl.BlockSpec((chunk, unit), lambda i, place: (i, 0))] * 8,
+            + [pl.BlockSpec((2, chunk, unit), lambda i, place: (0, i, 0))] * 2
+            + [pl.BlockSpec((chunk, unit), lambda i, place: (i, 0))] * 4,
             out_specs=pl.BlockSpec((count, 4 * unit), lambda i, place: (0, 0)),
             scratch_shapes=[pltpu.VMEM((count, 8 * unit), jnp.float32)],
         ),
@@ -112,44 +118,45 @@
     )(place, rows, *gates, *uppers)
 
 
-def down_kernel(place, mine, other, *refs):
-    weights, out = refs[0:4], refs[4]
+def down_kernel(place, hidden, own, far, out):
+    rows = hidden.shape[1]
+    unit = hidden.shape[2] // 4
     first = place[0] == 0
-    unit = mine.shape[1] // 4
-    total = None
-    for part in range(2):
-        own = mine[:, 2 * part * unit : (2 * part + 2) * unit]
-        far = other[:, 2 * part * unit : (2 * part + 2) * unit]
-        hidden = jnp.concatenate([jnp.where(first, own, far), jnp.where(first, far, own)], axis=1)
-        columns = jnp.concatenate([weights[2 * part][0], weights[2 * part + 1][0]], axis=1)
-        product = jnp.dot(hidden, columns, preferred_element_type=jnp.float32)
-        total = product if total is None else total + product
-    total = total.astype(jnp.bfloat16)
-    width = total.shape[1] // 2
-    out[place[1]] = total[:, :width]
-    out[1 - place[1]] = total[:, width:]
-
-
-def down(place, mine, other, weights):
-    count = mine.shape[0]
-    groups, depth, unit = weights[0].shape
+    step = pl.program_id(0)
+    for parity in range(2):
+        pieces = []
+        for part in range(2):
+            for high in range(2):
+                pieces.append(hidden[2 * high + parity, :, 2 * part * unit : (2 * part + 2) * unit])
+        own_hidden = jnp.concatenate(pieces[0:2], axis=1)
+        far_hidden = jnp.concatenate(pieces[2:4], axis=1)
+        own_columns = jnp.concatenate([own[0], own[1]], axis=1)
+        far_columns = jnp.concatenate([far[0], far[1]], axis=1)
+        total = jnp.dot(own_hidden, own_columns, preferred_element_type=jnp.float32)
+        total += jnp.dot(far_hidden, far_columns, preferred_element_type=jnp.float32)
+        out[parity] = total.astype(jnp.bfloat16)
+
+
+def down(place, hidden, own, far):
+    count = hidden.shape[1]
+    groups, depth, unit = own.shape
     return pl.pallas_call(
         down_kernel,
         out_shape=jax.ShapeDtypeStruct((2, count, groups * unit), jnp.bfloat16),
         grid_spec=pltpu.PrefetchScalarGridSpec(
             num_scalar_prefetch=1,
-            grid=(groups,),
-            in_specs=[pl.BlockSpec(mine.shape, lambda i, place: (0, 0))] * 2
-            + [pl.BlockSpec((1, depth, unit), lambda i, place: (i, 0, 0))] * 4,
-            out_specs=pl.BlockSpec((2, count, unit), lambda i, place: (0, 0, i)),
+            grid=(groups // 2,),
+            in_specs=[pl.BlockSpec(hidden.shape, lambda i, place: (0, 0, 0))]
+            + [pl.BlockSpec((2, depth, unit), lambda i, place: (i, 0, 0))] * 2,
+            out_specs=pl.BlockSpec((2, count, 2 * unit), lambda i, place: (0, 0, i)),
         ),
         compiler_params=pltpu.CompilerParams(vmem_limit_bytes=32 * 1024 * 1024),
         cost_estimate=pl.CostEstimate(
-            flops=2 * count * 2 * depth * 2 * groups * unit,
-            bytes_accessed=2 * (2 * count * mine.shape[1] + 4 * groups * depth * unit),
+            flops=2 * 2 * count * 2 * depth * groups * unit,
+            bytes_accessed=2 * (hidden.size + 2 * own.size + 2 * count * groups * unit),
             transcendentals=0,
         ),
-    )(place, mine, other, *weights)
+    )(place, hidden, own, far)
 
 
 def shards(queries, keys, values, residual, gain, expert_ids, gate_weights, w_gate, w_up, w_down):
@@ -166,23 +173,20 @@
     key_part = lax.dynamic_slice_in_dim(keys, head, HEAD_DIM, 1)
     value_part = lax.dynamic_slice_in_dim(values, head, HEAD_DIM, 1)
     sent = jnp.where(core == 0, key_part, value_part)
+    gate_own = lax.all_gather(w_gate[0], "ya")
     held = lax.all_to_all(
         jnp.broadcast_to(sent[None], (ctx_count, seq_rows, HEAD_DIM)), CTX, 0, 0, tiled=True
     ).reshape(ctx_count * seq_rows, HEAD_DIM)
+    w_up, w_down, held = lax.optimization_barrier((w_up, w_down, held))
+    up_side = swap(w_up[0], "ya")
     far = swap(held, "k")
     all_keys = jnp.where(core == 0, held, far)
     all_values = jnp.where(core == 0, far, held)
 
-    def four(own):
-        side = swap(own, "ya")
-        return [own, side, swap(own, "k"), swap(side, "k")]
-
-    gates = four(w_gate[0])
-    uppers = four(w_up[0])
     unit = w_down.shape[2]
     cut = w_down[0].reshape(ctx_count // z_count, z_count, unit, unit)
     cut = jnp.transpose(cut, (1, 0, 2, 3)).reshape(z_count, ctx_count // z_count * unit, unit)
-    downs = four(lax.all_to_all(cut, "z", 0, 0, tiled=True))
+    down_own = lax.all_to_all(cut, "z", 0, 0, tiled=True)
 
     heads = attention(queries, all_keys, all_values, ctx_index * seq_rows)
     stream = (residual.astype(jnp.float32) + heads.astype(jnp.float32)).astype(jnp.bfloat16)
@@ -214,16 +218,20 @@
     piece = jnp.transpose(normed, (0, 2, 1, 3)).reshape(CAP, exp_count * width)
 
     all_rows = lax.all_gather(piece, "z", axis=0, tiled=True)
+
+    gates = [gate_own, swap(gate_own, "k")]
+    uppers = [w_up[0], up_side, swap(w_up[0], "k"), swap(up_side, "k")]
     hidden = gate_up(place, all_rows, gates, uppers)
-    out = down(place, hidden, swap(hidden, "yp"), downs)
-
-    half_columns = out.shape[2]
-    back = out.reshape(2, z_count, 2, HALF, half_columns)
-    back = jnp.transpose(back, (2, 1, 0, 3, 4)).reshape(2 * z_count, 2, HALF, half_columns)
-    back = lax.all_to_all(back, ("yp", "z"), 0, 0, tiled=True)
-    back = back.reshape(2, z_count, 2, HALF, half_columns).astype(jnp.float32)
+    hidden = lax.all_gather(hidden, ("yp", "ya"))
+    out = down(place, hidden, down_own, swap(down_own, "k"))
+
+    columns = out.shape[2]
+    back = out.reshape(2, z_count, 2, HALF, columns)
+    back = jnp.transpose(back, (2, 0, 1, 3, 4)).reshape(ctx_count, HALF, columns)
+    back = lax.all_to_all(back, CTX, 0, 0, tiled=True)
+    back = back.reshape(ctx_count // z_count, z_count, HALF, columns).astype(jnp.float32)
     summed = jnp.sum(back, axis=1).astype(jnp.bfloat16)
-    summed = summed.reshape(4, HALF, half_columns // width, width)
+    summed = summed.reshape(ctx_count // z_count, HALF, columns // width, width)
     summed = jnp.transpose(summed, (0, 2, 1, 3)).reshape(exp_count, HALF, width)
     summed = jnp.pad(summed, ((0, 0), (0, PAD - HALF), (0, 0)))
     returned = lax.all_to_all(summed, EXP, 0, 0, tiled=True).reshape(table_rows, width)

time: 240 us -> 208 us (0.87)
  blocking collectives: 29.4 us -> 68.6 us
  waiting for transfers between devices: 92.8 us -> 54.7 us
  starting transfers between devices: 69 us -> 48 us
  local copies, waits for them, and re-layouts: 15.7 us -> 8.47 us
  Pallas kernels: 13.4 us -> 9.1 us
    all_to_all x2 -> x1, waiting for transfers between devices: 34.4 us -> 3.44 us  [shards(): down_own = lax.all_to_all(cut, 'z', 0, 0, tiled=True)]
    all_to_all x1 -> x2, blocking collectives: 29.4 us -> 52.8 us  [the longest x1 29.8 us: shards(): back = lax.all_to_all(back, CTX, 0, 0, tiled=True)]
    ppermute x11 -> x6, waiting for transfers between devices: 34.4 us -> 18 us  [swap(): return lax.ppermute(value, axis, SWAP)]
    ppermute x11 -> x6, starting transfers between devices: 36.7 us -> 20.6 us  [swap(): return lax.ppermute(value, axis, SWAP)]
    all_gather x0 -> x1, blocking collectives: none -> 15.9 us  [shards(): hidden = lax.all_gather(hidden, ('yp', 'ya'))]
    all_gather x1, waiting for transfers between devices: 0.01 us -> 9.3 us  [shards(): all_rows = lax.all_gather(piece, 'z', axis=0, tiled=True)]
    all_to_all x2 -> x1, starting transfers between devices: 11.3 us -> 3.88 us  [shards(): down_own = lax.all_to_all(cut, 'z', 0, 0, tiled=True)]
    unnamed x34 -> x23, local copies, waits for them, and re-layouts: 9.23 us -> 3.94 us
  transfers between devices with their start and end apart: 16 -> 11, of which waited for: 8 -> 6; matrix products, arithmetic and copies ran while one was open for 1% -> 2% of each run, Pallas kernels for 3% -> 3%
where the time goes in v2:
time: 208 us; the launch traced here: 207 us
  blocking collectives  68.6 us (33%)
  waiting for transfers between devices  54.7 us (26%)
  starting transfers between devices  48 us (23%)
  between operations  13.8 us (7%)
  Pallas kernels  9.1 us (4%)
  local copies, waits for them, and re-layouts  8.47 us (4%)
  matrix products  2.13 us (1%)
    all_to_all x1, blocking collectives, shards(): back = lax.all_to_all(back, CTX, 0, 0, tiled=True)  29.8 us
    all_to_all x1, blocking collectives, shards(): arrived = lax.all_to_all(outgoing, ('yp',) + EXP, 0, 0, tiled=True)  22.9 us
    ppermute x6, starting transfers between devices, swap(): return lax.ppermute(value, axis, SWAP)  20.6 us
    ppermute x6, waiting for transfers between devices, swap(): return lax.ppermute(value, axis, SWAP)  18 us
    all_gather x1, blocking collectives, shards(): hidden = lax.all_gather(hidden, ('yp', 'ya'))  15.9 us
    all_to_all x1, starting transfers between devices, shards(): lax.all_to_all(jnp.broadcast_to(sent[None], (ctx_count, seq_rows, HEAD_DI...  14.3 us
    all_to_all x1, waiting for transfers between devices, shards(): lax.all_to_all(jnp.broadcast_to(sent[None], (ctx_count, seq_rows, HEAD_DI...  13.2 us
    all_to_all x1, waiting for transfers between devices, shards(): lax.all_to_all(summed, EXP, 0, 0, tiled=True).reshape(table_rows, width)  10.1 us
  transfers between devices with their start and end apart: 11, of which 6 were waited for; matrix products, arithmetic and copies ran while one was open for 2% of the time, Pallas kernels for 3%

profile of v2, /device:TPU:1, one launch (start us, length us, event | category | flops | bytes accessed | tf_op | source)
XLA Modules:
  0.0 206.7 jit_solution(5374741976562270129)
XLA Ops:
  6.5 0.8 dynamic-slice_select_fusion
  7.3 0.9 broadcast_in_dim.64
  8.2 14.3 %all-to-all-start = ((bf16[32,64,128]{2,1,0:T(8,128)(2,1)}), bf16[32,64,128]{2,1,0:T(8,128)(2,1)S(1)}, u32[]{:S(2)}, u32[]{:S(2)}) async-start(bf16[32,64,128]{2,1,0:T(8,128)(2,1)} %broadcast_in_dim.64), calls=%async_computation | async-start | bytes 1048576 | tf_op jit(solution)/shard_map/all_to_all | solution.py:177
  22.6 0.7 all-gather.6.cloned.1.call-update
  24.2 13.2 %all-to-all-done = bf16[32,64,128]{2,1,0:T(8,128)(2,1)S(1)} async-done(((bf16[32,64,128]{2,1,0:T(8,128)(2,1)}), bf16[32,64,128]{2,1,0:T(8,128)(2,1)S(1)}, u32[]{:S(2)}, u32[]{:S(2)}) %all-to-all-start) | async-done | bytes 524320 | tf_op jit(solution)/shard_map/all_to_all | solution.py:177
  37.4 4.8 %collective-permute-start = (bf16[2048,128]{1,0:T(8,128)(2,1)S(1)}, bf16[2048,128]{1,0:T(8,128)(2,1)S(1)}, u32[]{:S(2)}, u32[]{:S(2)}) collective-permute-start(bf16[2048,128]{1,0:T(8,128)(2,1)S(1)} %bitcast.59), channel_id=1, source_target_pairs={{0,1},{1,0},{2,3},{3,2},{4,5},{5,4},{6,7},{7,6},{8,9},{9,8},{10,11... | collective-permute-start | bytes 1572872 | tf_op jit(solution)/shard_map/ppermute | solution.py:28
  42.4 1.3 collective-permute-done
  43.7 0.4 fusion.49
  44.5 0.4 fusion.2
  45.2 22.9 %all_to_all.25 = bf16[32,16,256]{2,1,0:T(8,128)(2,1)S(1)} all-to-all(bf16[32,16,256]{2,1,0:T(8,128)(2,1)S(1)} %bitcast.56), channel_id=1, replica_groups=mesh['yp'=2,'ya'=2,'z'=8,'x'=4,'h'=2,'k'=2] {'yp','x','h','k'}, dimensions={0} | all-to-all | bytes 524288 | tf_op jit(solution)/shard_map/all_to_all | solution.py:210
  68.6 0.7 copy.46
  69.4 1.0 copy.31
  70.4 3.9 %all-to-all-start.2 = ((bf16[8,512,128]{2,1,0:T(8,128)(2,1)}), bf16[8,512,128]{2,1,0:T(8,128)(2,1)S(1)}, u32[]{:S(2)}, u32[]{:S(2)}) async-start(bf16[8,512,128]{2,1,0:T(8,128)(2,1)} %bitcast.19), calls=%async_computation.2 | async-start | bytes 2097152 | tf_op jit(solution)/shard_map/all_to_all | solution.py:189
  74.3 2.7 %collective-permute-start.2 = (bf16[4096,128]{1,0:T(8,128)(2,1)}, bf16[4096,128]{1,0:T(8,128)(2,1)}, u32[]{:S(2)}, u32[]{:S(2)}) collective-permute-start(bf16[4096,128]{1,0:T(8,128)(2,1)} %bitcast.15.refs_0_), channel_id=1, source_target_pairs={{0,128},{128,0},{1,129},{129,1},{2,130},{130,2},{3,131},{131,3},{4... | collective-permute-start | bytes 3145736 | tf_op jit(solution)/shard_map/ppermute | solution.py:28
  77.0 4.2 %collective-permute-start.1 = (bf16[2,4096,128]{2,1,0:T(8,128)(2,1)}, bf16[2,4096,128]{2,1,0:T(8,128)(2,1)S(1)}, u32[]{:S(2)}, u32[]{:S(2)}) collective-permute-start(bf16[2,4096,128]{2,1,0:T(8,128)(2,1)} %all-gather.6.cloned.1.call-done.gate_own), channel_id=1, source_target_pairs={{0,1},{1,0},{2,3},{3,2},{4,5},{5,4},{6,7},{7,6},{8,9},{9,8},{10,11... | collective-permute-start | bytes 6291464 | tf_op jit(solution)/shard_map/ppermute | solution.py:28
  81.2 1.9 collective-permute-start.3
  83.1 16.7 %collective-permute-done.2.refs_1_ = bf16[4096,128]{1,0:T(8,128)(2,1)} collective-permute-done((bf16[4096,128]{1,0:T(8,128)(2,1)}, bf16[4096,128]{1,0:T(8,128)(2,1)}, u32[]{:S(2)}, u32[]{:S(2)}) %collective-permute-start.2) | collective-permute-done | bytes 1048608 | tf_op jit(solution)/shard_map/ppermute | solution.py:28
  99.8 4.2 %collective-permute-start.4 = (bf16[4096,128]{1,0:T(8,128)(2,1)}, bf16[4096,128]{1,0:T(8,128)(2,1)}, u32[]{:S(2)}, u32[]{:S(2)}) collective-permute-start(bf16[4096,128]{1,0:T(8,128)(2,1)} %collective-permute-done.2.refs_1_), channel_id=1, source_target_pairs={{0,1},{1,0},{2,3},{3,2},{4,5},{5,4},{6,7},{7,6},{8,9},{9,8},{10,11... | collective-permute-start | bytes 3145736 | tf_op jit(solution)/shard_map/ppermute | solution.py:28
  104.0 3.4 %all-to-all-done.2.own = bf16[8,512,128]{2,1,0:T(8,128)(2,1)S(1)} async-done(((bf16[8,512,128]{2,1,0:T(8,128)(2,1)}), bf16[8,512,128]{2,1,0:T(8,128)(2,1)S(1)}, u32[]{:S(2)}, u32[]{:S(2)}) %all-to-all-start.2) | async-done | bytes 1048608 | tf_op jit(solution)/shard_map/all_to_all | solution.py:189
  107.4 2.9 %collective-permute-start.5 = (bf16[8,512,128]{2,1,0:T(8,128)(2,1)S(1)}, bf16[8,512,128]{2,1,0:T(8,128)(2,1)}, u32[]{:S(2)}, u32[]{:S(2)}) collective-permute-start(bf16[8,512,128]{2,1,0:T(8,128)(2,1)S(1)} %all-to-all-done.2.own), channel_id=1, source_target_pairs={{0,1},{1,0},{2,3},{3,2},{4,5},{5,4},{6,7},{7,6},{8,9},{9,8},{10,11... | collective-permute-start | bytes 3145736 | tf_op jit(solution)/shard_map/ppermute | solution.py:28
  110.4 9.3 %all-gather.4.cloned.1.call-done.rows = bf16[192,4096]{1,0:T(8,128)(2,1)} async-done(((bf16[24,4096]{1,0:T(8,128)(2,1)}), bf16[192,4096]{1,0:T(8,128)(2,1)}) %all-gather.4.cloned.1.call-update) | async-done | bytes 1572880 | tf_op jit(solution)/shard_map/all_gather | solution.py:220
  119.7 1.6 copy-done.1
  121.3 1.4 copy-done.2
  122.7 5.4 %shard_map.100 = bf16[192,512]{1,0:T(8,128)(2,1)S(1)} custom-call(s32[2]{0:T(128)S(1)} %pad_add_fusion.place, bf16[192,4096]{1,0:T(8,128)(2,1)S(1)} %copy-done.2, bf16[2,4096,128]{2,1,0:T(8,128)(2,1)S(1)} %copy-done.1, bf16[2,4096,128]{2,1,0:T(8,128)(2,1)S(1)} %collective-permute-done.1.gate_far, bf16[4096,128]{1,0:T(8,128)(2,1)} %bitcast.15.refs_0_, ...), custom_call_target="tpu_custom_call" | custom-call | flops 1610612736 | bytes 9961472 | tf_op jit(solution)/shard_map/pallas_call | solution.py:100
  128.2 15.9 %all-gather = bf16[768,512]{1,0:T(8,128)(2,1)S(1)} all-gather(bf16[192,512]{1,0:T(8,128)(2,1)S(1)} %shard_map.100), channel_id=2, replica_groups=mesh['yp'=2,'ya'=2,'z'=8,'x'=4,'h'=2,'k'=2] {'yp','ya'}, dimensions={0}, use_global_device_ids=true | all-gather | bytes 983040 | tf_op jit(solution)/shard_map/all_gather | solution.py:225
  144.0 3.7 %shard_map.101 = bf16[2,192,1024]{2,1,0:T(8,128)(2,1)S(1)} custom-call(s32[2]{0:T(128)S(1)} %pad_add_fusion.place, bf16[4,192,512]{2,1,0:T(8,128)(2,1)S(1)} %bitcast.52, bf16[8,512,128]{2,1,0:T(8,128)(2,1)S(1)} %all-to-all-done.2.own, bf16[8,512,128]{2,1,0:T(8,128)(2,1)} %collective-permute-done.5.far), custom_call_target="tpu_custom_call" | custom-call | flops 805306368 | bytes 3670016 | tf_op jit(solution)/shard_map/pallas_call | solution.py:143
  147.7 0.8 copy.32
  148.8 29.8 %all_to_all.26 = bf16[32,12,1024]{2,1,0:T(8,128)(2,1)S(1)} all-to-all(bf16[32,12,1024]{2,1,0:T(8,128)(2,1)S(1)} %bitcast.53), channel_id=1, replica_groups=mesh['yp'=2,'ya'=2,'z'=8,'x'=4,'h'=2,'k'=2] {'yp','ya','z'}, dimensions={0} | all-to-all | bytes 1572864 | tf_op jit(solution)/shard_map/all_to_all | solution.py:231
  179.0 0.7 pad.4
  179.7 9.1 %all-to-all-start.4 = ((bf16[16,16,256]{2,1,0:T(8,128)(2,1)}), bf16[16,16,256]{2,1,0:T(8,128)(2,1)S(1)}, u32[]{:S(2)}, u32[]{:S(2)}) async-start(bf16[16,16,256]{2,1,0:T(8,128)(2,1)} %pad.4), calls=%async_computation.4 | async-start | bytes 262144 | tf_op jit(solution)/shard_map/all_to_all | solution.py:237
  188.9 10.1 %all-to-all-done.4 = bf16[16,16,256]{2,1,0:T(8,128)(2,1)S(1)} async-done(((bf16[16,16,256]{2,1,0:T(8,128)(2,1)}), bf16[16,16,256]{2,1,0:T(8,128)(2,1)S(1)}, u32[]{:S(2)}, u32[]{:S(2)}) %all-to-all-start.4) | async-done | bytes 131104 | tf_op jit(solution)/shard_map/all_to_all | solution.py:237
  199.0 0.9 fusion.3
  (63 shorter events, 2.9 us)
Async XLA Ops:
  6.5 16.8 %copy-start = (s32[2048,2]{0,1:T(2,128)S(1)}, s32[2048,2]{0,1:T(2,128)}, u32[]{:S(2)}) copy-start(s32[2048,2]{0,1:T(2,128)} %param.15) | copy-start | bytes 49156
  6.5 16.8 %copy-start.5 = (bf16[64,256]{1,0:T(8,128)(2,1)S(1)}, bf16[64,256]{1,0:T(8,128)(2,1)}, u32[]{:S(2)}) copy-start(bf16[64,256]{1,0:T(8,128)(2,1)} %param.10) | copy-start | bytes 98308
  6.5 17.5 %copy-start.7 = (bf16[256]{0:T(256)(128)(2,1)S(1)}, bf16[256]{0:T(256)(128)(2,1)}, u32[]{:S(2)}) copy-start(bf16[256]{0:T(256)(128)(2,1)} %param.14) | copy-start | bytes 1540
  8.2 29.2 %all-to-all-start = ((bf16[32,64,128]{2,1,0:T(8,128)(2,1)}), bf16[32,64,128]{2,1,0:T(8,128)(2,1)S(1)}, u32[]{:S(2)}, u32[]{:S(2)}) async-start(bf16[32,64,128]{2,1,0:T(8,128)(2,1)} %broadcast_in_dim.64), calls=%async_computation | async-start | bytes 1048576 | tf_op jit(solution)/shard_map/all_to_all | solution.py:177
  22.5 54.5 %all-gather.6.cloned.1.call-start = ((), (), s32[]{:S(2)}) async-start(), calls=%async_computation.6 | async-start | bytes 3145728 | tf_op jit(solution)/shard_map/all_gather | solution.py:176
  23.3 96.5 %all-gather.4.cloned.1.call-start = ((), (), s32[]{:S(2)}) async-start(), calls=%async_computation.5 | async-start | bytes 1769472 | tf_op jit(solution)/shard_map/all_gather | solution.py:220
  37.4 6.3 %collective-permute-start = (bf16[2048,128]{1,0:T(8,128)(2,1)S(1)}, bf16[2048,128]{1,0:T(8,128)(2,1)S(1)}, u32[]{:S(2)}, u32[]{:S(2)}) collective-permute-start(bf16[2048,128]{1,0:T(8,128)(2,1)S(1)} %bitcast.59), channel_id=1, source_target_pairs={{0,1},{1,0},{2,3},{3,2},{4,5},{5,4},{6,7},{7,6},{8,9},{9,8},{10,11... | collective-permute-start | bytes 1572872 | tf_op jit(solution)/shard_map/ppermute | solution.py:28
  44.2 0.8 copy-start.4
  45.2 24.2 %copy-start.3 = (bf16[1,4096,128]{2,1,0:T(8,128)(2,1)S(1)}, bf16[1,4096,128]{2,1,0:T(8,128)(2,1)}, u32[]{:S(2)}) copy-start(bf16[1,4096,128]{2,1,0:T(8,128)(2,1)} %param.19) | copy-start | bytes 3145732
  70.4 37.0 %all-to-all-start.2 = ((bf16[8,512,128]{2,1,0:T(8,128)(2,1)}), bf16[8,512,128]{2,1,0:T(8,128)(2,1)S(1)}, u32[]{:S(2)}, u32[]{:S(2)}) async-start(bf16[8,512,128]{2,1,0:T(8,128)(2,1)} %bitcast.19), calls=%async_computation.2 | async-start | bytes 2097152 | tf_op jit(solution)/shard_map/all_to_all | solution.py:189
  74.3 25.5 %collective-permute-start.2 = (bf16[4096,128]{1,0:T(8,128)(2,1)}, bf16[4096,128]{1,0:T(8,128)(2,1)}, u32[]{:S(2)}, u32[]{:S(2)}) collective-permute-start(bf16[4096,128]{1,0:T(8,128)(2,1)} %bitcast.15.refs_0_), channel_id=1, source_target_pairs={{0,128},{128,0},{1,129},{129,1},{2,130},{130,2},{3,131},{131,3},{4... | collective-permute-start | bytes 3145736 | tf_op jit(solution)/shard_map/ppermute | solution.py:28
  77.0 33.4 %collective-permute-start.1 = (bf16[2,4096,128]{2,1,0:T(8,128)(2,1)}, bf16[2,4096,128]{2,1,0:T(8,128)(2,1)S(1)}, u32[]{:S(2)}, u32[]{:S(2)}) collective-permute-start(bf16[2,4096,128]{2,1,0:T(8,128)(2,1)} %all-gather.6.cloned.1.call-done.gate_own), channel_id=1, source_target_pairs={{0,1},{1,0},{2,3},{3,2},{4,5},{5,4},{6,7},{7,6},{8,9},{9,8},{10,11... | collective-permute-start | bytes 6291464 | tf_op jit(solution)/shard_map/ppermute | solution.py:28
  81.2 29.2 %collective-permute-start.3 = (bf16[4096,128]{1,0:T(8,128)(2,1)}, bf16[4096,128]{1,0:T(8,128)(2,1)}, u32[]{:S(2)}, u32[]{:S(2)}) collective-permute-start(bf16[4096,128]{1,0:T(8,128)(2,1)} %bitcast.15.refs_0_), channel_id=1, source_target_pairs={{0,1},{1,0},{2,3},{3,2},{4,5},{5,4},{6,7},{7,6},{8,9},{9,8},{10,11... | collective-permute-start | bytes 3145736 | tf_op jit(solution)/shard_map/ppermute | solution.py:28
  99.8 10.6 %collective-permute-start.4 = (bf16[4096,128]{1,0:T(8,128)(2,1)}, bf16[4096,128]{1,0:T(8,128)(2,1)}, u32[]{:S(2)}, u32[]{:S(2)}) collective-permute-start(bf16[4096,128]{1,0:T(8,128)(2,1)} %collective-permute-done.2.refs_1_), channel_id=1, source_target_pairs={{0,1},{1,0},{2,3},{3,2},{4,5},{5,4},{6,7},{7,6},{8,9},{9,8},{10,11... | collective-permute-start | bytes 3145736 | tf_op jit(solution)/shard_map/ppermute | solution.py:28
  107.4 36.6 %collective-permute-start.5 = (bf16[8,512,128]{2,1,0:T(8,128)(2,1)S(1)}, bf16[8,512,128]{2,1,0:T(8,128)(2,1)}, u32[]{:S(2)}, u32[]{:S(2)}) collective-permute-start(bf16[8,512,128]{2,1,0:T(8,128)(2,1)S(1)} %all-to-all-done.2.own), channel_id=1, source_target_pairs={{0,1},{1,0},{2,3},{3,2},{4,5},{5,4},{6,7},{7,6},{8,9},{9,8},{10,11... | collective-permute-start | bytes 3145736 | tf_op jit(solution)/shard_map/ppermute | solution.py:28
  119.7 1.6 copy-start.1
  121.3 1.4 copy-start.2
  148.7 40.1 %copy-start.6 = (f32[64,2]{0,1:T(2,128)S(1)}, f32[64,2]{0,1:T(2,128)}, u32[]{:S(2)}) copy-start(f32[64,2]{0,1:T(2,128)} %param.16) | copy-start | bytes 1540
  179.7 19.3 %all-to-all-start.4 = ((bf16[16,16,256]{2,1,0:T(8,128)(2,1)}), bf16[16,16,256]{2,1,0:T(8,128)(2,1)S(1)}, u32[]{:S(2)}, u32[]{:S(2)}) async-start(bf16[16,16,256]{2,1,0:T(8,128)(2,1)} %pad.4), calls=%async_computation.4 | async-start | bytes 262144 | tf_op jit(solution)/shard_map/all_to_all | solution.py:237
Sparse Core Ops, SparseCore 0:
  25.5 45.7 all-gather.5
  73.3 46.3 all-gather.3

commit v3 on v2

--- a/solution.py
+++ b/solution.py
@@ -96,7 +96,7 @@
 def gate_up(place, rows, gates, uppers):
     count, depth = rows.shape
     unit = uppers[0].shape[1]
-    chunk = 1024
+    chunk = 2048
     return pl.pallas_call(
         gate_up_kernel,
         out_shape=jax.ShapeDtypeStruct((count, 4 * unit), jnp.bfloat16),
@@ -109,7 +109,7 @@
             out_specs=pl.BlockSpec((count, 4 * unit), lambda i, place: (0, 0)),
             scratch_shapes=[pltpu.VMEM((count, 8 * unit), jnp.float32)],
         ),
-        compiler_params=pltpu.CompilerParams(vmem_limit_bytes=32 * 1024 * 1024),
+        compiler_params=pltpu.CompilerParams(vmem_limit_bytes=60 * 1024 * 1024),
         cost_estimate=pl.CostEstimate(
             flops=2 * count * depth * 8 * unit,
             bytes_accessed=2 * depth * (count + 8 * unit),
@@ -118,45 +118,59 @@
     )(place, rows, *gates, *uppers)
 
 
-def down_kernel(place, hidden, own, far, out):
+def down_kernel(hidden, own, far, out, product, sorted_rows):
     rows = hidden.shape[1]
-    unit = hidden.shape[2] // 4
-    first = place[0] == 0
-    step = pl.program_id(0)
-    for parity in range(2):
-        pieces = []
-        for part in range(2):
-            for high in range(2):
-                pieces.append(hidden[2 * high + parity, :, 2 * part * unit : (2 * part + 2) * unit])
-        own_hidden = jnp.concatenate(pieces[0:2], axis=1)
-        far_hidden = jnp.concatenate(pieces[2:4], axis=1)
-        own_columns = jnp.concatenate([own[0], own[1]], axis=1)
-        far_columns = jnp.concatenate([far[0], far[1]], axis=1)
-        total = jnp.dot(own_hidden, own_columns, preferred_element_type=jnp.float32)
-        total += jnp.dot(far_hidden, far_columns, preferred_element_type=jnp.float32)
-        out[parity] = total.astype(jnp.bfloat16)
-
-
-def down(place, hidden, own, far):
+    groups, _, unit = own.shape
+    blocks = out.shape[0] // 4
+    parts = []
+    for part in range(2):
+        at = slice(2 * part * unit, (2 * part + 2) * unit)
+        wide = [
+            jnp.concatenate([hidden[parity, :, at], hidden[2 + parity, :, at]], axis=1)
+            for parity in range(2)
+        ]
+        parts.append(jnp.concatenate(wide, axis=0))
+    for pair in range(0, groups, 2):
+        total = None
+        for part, weights in enumerate((own, far)):
+            columns = jnp.concatenate([weights[pair], weights[pair + 1]], axis=1)
+            term = jnp.dot(parts[part], columns, preferred_element_type=jnp.float32)
+            total = term if total is None else total + term
+        product[...] = total
+        for which in range(2):
+            lanes = slice(which * unit, (which + 1) * unit)
+            to = (pair + which) * HALF
+            for parity in range(2):
+                for z in range(blocks):
+                    at = parity * rows + z * CAP
+                    near, distant = parity * blocks + z, (2 + parity) * blocks + z
+                    sorted_rows[near, to : to + HALF] = product[at : at + HALF, lanes]
+                    sorted_rows[distant, to : to + HALF] = product[at + HALF : at + CAP, lanes]
+    out[...] = sorted_rows[...].astype(jnp.bfloat16)
+
+
+def down(hidden, own, far, blocks):
     count = hidden.shape[1]
     groups, depth, unit = own.shape
+    whole = lambda array: pl.BlockSpec(array.shape, lambda i: (0,) * len(array.shape))
+    result = jax.ShapeDtypeStruct((blocks, groups * HALF, unit), jnp.bfloat16)
     return pl.pallas_call(
         down_kernel,
-        out_shape=jax.ShapeDtypeStruct((2, count, groups * unit), jnp.bfloat16),
-        grid_spec=pltpu.PrefetchScalarGridSpec(
-            num_scalar_prefetch=1,
-            grid=(groups // 2,),
-            in_specs=[pl.BlockSpec(hidden.shape, lambda i, place: (0, 0, 0))]
-            + [pl.BlockSpec((2, depth, unit), lambda i, place: (i, 0, 0))] * 2,
-            out_specs=pl.BlockSpec((2, count, 2 * unit), lambda i, place: (0, 0, i)),
-        ),
+        out_shape=result,
+        grid=(1,),
+        in_specs=[whole(hidden), whole(own), whole(far)],
+        out_specs=whole(result),
+        scratch_shapes=[
+            pltpu.VMEM((2 * count, 2 * unit), jnp.float32),
+            pltpu.VMEM(result.shape, jnp.float32),
+        ],
         compiler_params=pltpu.CompilerParams(vmem_limit_bytes=32 * 1024 * 1024),
         cost_estimate=pl.CostEstimate(
             flops=2 * 2 * count * 2 * depth * groups * unit,
             bytes_accessed=2 * (hidden.size + 2 * own.size + 2 * count * groups * unit),
             transcendentals=0,
         ),
-    )(place, hidden, own, far)
+    )(hidden, own, far)
 
 
 def shards(queries, keys, values, residual, gain, expert_ids, gate_weights, w_gate, w_up, w_down):
@@ -186,7 +200,6 @@
     unit = w_down.shape[2]
     cut = w_down[0].reshape(ctx_count // z_count, z_count, unit, unit)
     cut = jnp.transpose(cut, (1, 0, 2, 3)).reshape(z_count, ctx_count // z_count * unit, unit)
-    down_own = lax.all_to_all(cut, "z", 0, 0, tiled=True)
 
     heads = attention(queries, all_keys, all_values, ctx_index * seq_rows)
     stream = (residual.astype(jnp.float32) + heads.astype(jnp.float32)).astype(jnp.bfloat16)
@@ -218,27 +231,31 @@
     piece = jnp.transpose(normed, (0, 2, 1, 3)).reshape(CAP, exp_count * width)
 
     all_rows = lax.all_gather(piece, "z", axis=0, tiled=True)
-
     gates = [gate_own, swap(gate_own, "k")]
     uppers = [w_up[0], up_side, swap(w_up[0], "k"), swap(up_side, "k")]
+    down_own = lax.all_to_all(cut, "z", 0, 0, tiled=True)
     hidden = gate_up(place, all_rows, gates, uppers)
     hidden = lax.all_gather(hidden, ("yp", "ya"))
-    out = down(place, hidden, down_own, swap(down_own, "k"))
-
-    columns = out.shape[2]
-    back = out.reshape(2, z_count, 2, HALF, columns)
-    back = jnp.transpose(back, (2, 0, 1, 3, 4)).reshape(ctx_count, HALF, columns)
+    back = down(hidden, down_own, swap(down_own, "k"), ctx_count)
     back = lax.all_to_all(back, CTX, 0, 0, tiled=True)
-    back = back.reshape(ctx_count // z_count, z_count, HALF, columns).astype(jnp.float32)
+    back = back.reshape(ctx_count // z_count, z_count, z_count * HALF, unit).astype(jnp.float32)
     summed = jnp.sum(back, axis=1).astype(jnp.bfloat16)
-    summed = summed.reshape(ctx_count // z_count, HALF, columns // width, width)
-    summed = jnp.transpose(summed, (0, 2, 1, 3)).reshape(exp_count, HALF, width)
-    summed = jnp.pad(summed, ((0, 0), (0, PAD - HALF), (0, 0)))
-    returned = lax.all_to_all(summed, EXP, 0, 0, tiled=True).reshape(table_rows, width)
-    mix = jnp.where(rows_of[:, 0:1] == row_id[None, :], gate_weights[:, 0:1], 0.0) + jnp.where(
-        rows_of[:, 1:2] == row_id[None, :], gate_weights[:, 1:2], 0.0
-    )
-    routed = jnp.dot(mix, returned.astype(jnp.float32), precision=lax.Precision.HIGHEST)
+    tall = width // unit * HALF
+    returned = lax.all_to_all(summed.reshape(exp_count, tall, unit), EXP, 0, 0, tiled=True)
+    returned = returned.reshape(exp_count * tall, unit).astype(jnp.float32)
+    place_of = rows_of // PAD * tall + rows_of % PAD
+    order = jnp.arange(exp_count * tall, dtype=jnp.int32)
+    mixes = []
+    for column in range(width // unit):
+        at = place_of + column * HALF
+        mixes.append(
+            jnp.where(at[:, 0:1] == order[None, :], gate_weights[:, 0:1], 0.0)
+            + jnp.where(at[:, 1:2] == order[None, :], gate_weights[:, 1:2], 0.0)
+        )
+    routed = jnp.dot(jnp.concatenate(mixes, axis=0), returned, precision=lax.Precision.HIGHEST)
+    routed = jnp.concatenate(
+        [routed[i * seq_rows : (i + 1) * seq_rows] for i in range(len(mixes))], axis=1
+    )
     return (stream.astype(jnp.float32) + routed).astype(jnp.bfloat16)
 
 

time: 208 us -> 197 us (0.947)
  blocking collectives: 68.6 us -> 38.4 us
  waiting for transfers between devices: 54.7 us -> 69.7 us
  starting transfers between devices: 48 us -> 57 us
  local copies, waits for them, and re-layouts: 8.47 us -> 3.97 us
    all_to_all x1 -> x0, blocking collectives: 29.8 us -> none  [shards(): back = lax.all_to_all(back, CTX, 0, 0, tiled=True)]
    all_to_all x1 -> x2, waiting for transfers between devices: 10.1 us -> 25.6 us  [the longest x1 16 us: shards(): back = lax.all_to_all(back, CTX, 0, 0, tiled=True)]
    all_to_all x1 -> x2, starting transfers between devices: 9.13 us -> 18.1 us  [the longest x1 11.4 us: shards(): lax.all_to_all(summed.reshape(exp_count, tall, unit), EXP, 0, 0, tiled=True)]
    unnamed x23 -> x17, local copies, waits for them, and re-layouts: 3.94 us -> 0.91 us
  transfers between devices with their start and end apart: 11 -> 12, of which waited for: 6 -> 7; matrix products, arithmetic and copies ran while one was open for 2% -> 3% of each run, Pallas kernels for 3% -> 3%
where the time goes in v3:
time: 197 us; the launch traced here: 196 us
  waiting for transfers between devices  69.7 us (35%)
  starting transfers between devices  57 us (29%)
  blocking collectives  38.4 us (19%)
  between operations  13.7 us (7%)
  Pallas kernels  8.39 us (4%)
  local copies, waits for them, and re-layouts  3.97 us (2%)
  other arithmetic  3.54 us (2%)
    all_to_all x1, blocking collectives, shards(): arrived = lax.all_to_all(outgoing, ('yp',) + EXP, 0, 0, tiled=True)  22.9 us
    ppermute x6, starting transfers between devices, swap(): return lax.ppermute(value, axis, SWAP)  20.6 us
    ppermute x6, waiting for transfers between devices, swap(): return lax.ppermute(value, axis, SWAP)  17.7 us
    all_to_all x1, waiting for transfers between devices, shards(): back = lax.all_to_all(back, CTX, 0, 0, tiled=True)  16 us
    all_gather x1, blocking collectives, shards(): hidden = lax.all_gather(hidden, ('yp', 'ya'))  15.5 us
    all_to_all x1, starting transfers between devices, shards(): lax.all_to_all(jnp.broadcast_to(sent[None], (ctx_count, seq_rows, HEAD_DI...  14.3 us
    all_to_all x1, waiting for transfers between devices, shards(): lax.all_to_all(jnp.broadcast_to(sent[None], (ctx_count, seq_rows, HEAD_DI...  13.2 us
    all_to_all x1, starting transfers between devices, shards(): lax.all_to_all(summed.reshape(exp_count, tall, unit), EXP, 0, 0, tiled=True)  11.4 us
  transfers between devices with their start and end apart: 12, of which 7 were waited for; matrix products, arithmetic and copies ran while one was open for 3% of the time, Pallas kernels for 3%

profile of v3, /device:TPU:1, one launch (start us, length us, event | category | flops | bytes accessed | tf_op | source)
XLA Modules:
  0.0 196.2 jit_solution(14102796191004365108)
XLA Ops:
  6.5 0.8 dynamic-slice_select_fusion
  7.3 0.9 broadcast_in_dim.74
  8.2 14.3 %all-to-all-start = ((bf16[32,64,128]{2,1,0:T(8,128)(2,1)}), bf16[32,64,128]{2,1,0:T(8,128)(2,1)S(1)}, u32[]{:S(2)}, u32[]{:S(2)}) async-start(bf16[32,64,128]{2,1,0:T(8,128)(2,1)} %broadcast_in_dim.74), calls=%async_computation | async-start | bytes 1048576 | tf_op jit(solution)/shard_map/all_to_all | solution.py:191
  22.6 0.7 all-gather.6.cloned.1.call-update
  24.2 13.2 %all-to-all-done = bf16[32,64,128]{2,1,0:T(8,128)(2,1)S(1)} async-done(((bf16[32,64,128]{2,1,0:T(8,128)(2,1)}), bf16[32,64,128]{2,1,0:T(8,128)(2,1)S(1)}, u32[]{:S(2)}, u32[]{:S(2)}) %all-to-all-start) | async-done | bytes 524320 | tf_op jit(solution)/shard_map/all_to_all | solution.py:191
  37.4 4.8 %collective-permute-start = (bf16[2048,128]{1,0:T(8,128)(2,1)S(1)}, bf16[2048,128]{1,0:T(8,128)(2,1)S(1)}, u32[]{:S(2)}, u32[]{:S(2)}) collective-permute-start(bf16[2048,128]{1,0:T(8,128)(2,1)S(1)} %bitcast.56), channel_id=1, source_target_pairs={{0,1},{1,0},{2,3},{3,2},{4,5},{5,4},{6,7},{7,6},{8,9},{9,8},{10,11... | collective-permute-start | bytes 1572872 | tf_op jit(solution)/shard_map/ppermute | solution.py:28
  42.5 1.2 collective-permute-done
  43.7 0.4 fusion.53
  44.1 0.3 fusion.4
  44.4 0.4 fusion.2
  45.2 22.9 %all_to_all.25 = bf16[32,16,256]{2,1,0:T(8,128)(2,1)S(1)} all-to-all(bf16[32,16,256]{2,1,0:T(8,128)(2,1)S(1)} %bitcast.53), channel_id=1, replica_groups=mesh['yp'=2,'ya'=2,'z'=8,'x'=4,'h'=2,'k'=2] {'yp','x','h','k'}, dimensions={0} | all-to-all | bytes 524288 | tf_op jit(solution)/shard_map/all_to_all | solution.py:223
  68.6 0.7 copy.31
  69.4 1.1 copy.27
  70.5 3.9 %all-to-all-start.2 = ((bf16[8,512,128]{2,1,0:T(8,128)(2,1)}), bf16[8,512,128]{2,1,0:T(8,128)(2,1)S(1)}, u32[]{:S(2)}, u32[]{:S(2)}) async-start(bf16[8,512,128]{2,1,0:T(8,128)(2,1)} %bitcast.19), calls=%async_computation.2 | async-start | bytes 2097152 | tf_op jit(solution)/shard_map/all_to_all | solution.py:236
  74.4 2.7 %collective-permute-start.2 = (bf16[4096,128]{1,0:T(8,128)(2,1)S(1)}, bf16[4096,128]{1,0:T(8,128)(2,1)}, u32[]{:S(2)}, u32[]{:S(2)}) collective-permute-start(bf16[4096,128]{1,0:T(8,128)(2,1)S(1)} %bitcast.50), channel_id=1, source_target_pairs={{0,128},{128,0},{1,129},{129,1},{2,130},{130,2},{3,131},{131,3},{4... | collective-permute-start | bytes 3145736 | tf_op jit(solution)/shard_map/ppermute | solution.py:28
  77.1 4.2 %collective-permute-start.1 = (bf16[2,4096,128]{2,1,0:T(8,128)(2,1)}, bf16[2,4096,128]{2,1,0:T(8,128)(2,1)}, u32[]{:S(2)}, u32[]{:S(2)}) collective-permute-start(bf16[2,4096,128]{2,1,0:T(8,128)(2,1)} %all-gather.6.cloned.1.call-done.gate_own), channel_id=1, source_target_pairs={{0,1},{1,0},{2,3},{3,2},{4,5},{5,4},{6,7},{7,6},{8,9},{9,8},{10,11... | collective-permute-start | bytes 6291464 | tf_op jit(solution)/shard_map/ppermute | solution.py:28
  81.3 1.9 collective-permute-start.3
  83.2 16.5 %collective-permute-done.2.refs_1_ = bf16[4096,128]{1,0:T(8,128)(2,1)} collective-permute-done((bf16[4096,128]{1,0:T(8,128)(2,1)S(1)}, bf16[4096,128]{1,0:T(8,128)(2,1)}, u32[]{:S(2)}, u32[]{:S(2)}) %collective-permute-start.2) | collective-permute-done | bytes 1048608 | tf_op jit(solution)/shard_map/ppermute | solution.py:28
  99.7 4.2 %collective-permute-start.4 = (bf16[4096,128]{1,0:T(8,128)(2,1)}, bf16[4096,128]{1,0:T(8,128)(2,1)}, u32[]{:S(2)}, u32[]{:S(2)}) collective-permute-start(bf16[4096,128]{1,0:T(8,128)(2,1)} %collective-permute-done.2.refs_1_), channel_id=1, source_target_pairs={{0,1},{1,0},{2,3},{3,2},{4,5},{5,4},{6,7},{7,6},{8,9},{9,8},{10,11... | collective-permute-start | bytes 3145736 | tf_op jit(solution)/shard_map/ppermute | solution.py:28
  103.9 3.8 %all-to-all-done.2.own = bf16[8,512,128]{2,1,0:T(8,128)(2,1)S(1)} async-done(((bf16[8,512,128]{2,1,0:T(8,128)(2,1)}), bf16[8,512,128]{2,1,0:T(8,128)(2,1)S(1)}, u32[]{:S(2)}, u32[]{:S(2)}) %all-to-all-start.2) | async-done | bytes 1048608 | tf_op jit(solution)/shard_map/all_to_all | solution.py:236
  107.7 2.9 %collective-permute-start.5 = (bf16[8,512,128]{2,1,0:T(8,128)(2,1)S(1)}, bf16[8,512,128]{2,1,0:T(8,128)(2,1)S(1)}, u32[]{:S(2)}, u32[]{:S(2)}) collective-permute-start(bf16[8,512,128]{2,1,0:T(8,128)(2,1)S(1)} %all-to-all-done.2.own), channel_id=1, source_target_pairs={{0,1},{1,0},{2,3},{3,2},{4,5},{5,4},{6,7},{7,6},{8,9},{9,8},{10,11... | collective-permute-start | bytes 3145736 | tf_op jit(solution)/shard_map/ppermute | solution.py:28
  110.6 0.6 pad_add_fusion.place
  111.1 8.7 %all-gather.4.cloned.1.call-done.rows = bf16[192,4096]{1,0:T(8,128)(2,1)} async-done(((bf16[24,4096]{1,0:T(8,128)(2,1)}), bf16[192,4096]{1,0:T(8,128)(2,1)}) %all-gather.4.cloned.1.call-update) | async-done | bytes 1572880 | tf_op jit(solution)/shard_map/all_gather | solution.py:233
  119.8 6.4 %shard_map.100 = bf16[192,512]{1,0:T(8,128)(2,1)} custom-call(s32[2]{0:T(128)} %pad_add_fusion.place, bf16[192,4096]{1,0:T(8,128)(2,1)} %all-gather.4.cloned.1.call-done.rows, bf16[2,4096,128]{2,1,0:T(8,128)(2,1)} %all-gather.6.cloned.1.call-done.gate_own, bf16[2,4096,128]{2,1,0:T(8,128)(2,1)} %collective-permute-done.1.gate_far, ...), custom_call_target="tpu_custom_call" | custom-call | flops 1610612736 | bytes 9961472 | tf_op jit(solution)/shard_map/pallas_call | solution.py:100
  126.2 15.5 %all-gather = bf16[768,512]{1,0:T(8,128)(2,1)S(1)} all-gather(bf16[192,512]{1,0:T(8,128)(2,1)} %shard_map.100), channel_id=2, replica_groups=mesh['yp'=2,'ya'=2,'z'=8,'x'=4,'h'=2,'k'=2] {'yp','ya'}, dimensions={0}, use_global_device_ids=true | all-gather | bytes 983040 | tf_op jit(solution)/shard_map/all_gather | solution.py:238
  141.7 2.0 %shard_map.101 = bf16[32,96,128]{2,1,0:T(8,128)(2,1)} custom-call(bf16[4,192,512]{2,1,0:T(8,128)(2,1)S(1)} %bitcast.48, bf16[8,512,128]{2,1,0:T(8,128)(2,1)S(1)} %all-to-all-done.2.own, bf16[8,512,128]{2,1,0:T(8,128)(2,1)S(1)} %collective-permute-done.5.far), custom_call_target="tpu_custom_call" | custom-call | flops 805306368 | bytes 3670016 | tf_op jit(solution)/shard_map/pallas_call | solution.py:157
  143.7 6.7 %all-to-all-start.3 = ((bf16[32,96,128]{2,1,0:T(8,128)(2,1)}), bf16[32,96,128]{2,1,0:T(8,128)(2,1)S(1)}, u32[]{:S(2)}, u32[]{:S(2)}) async-start(bf16[32,96,128]{2,1,0:T(8,128)(2,1)} %shard_map.101), calls=%async_computation.3 | async-start | bytes 1572864 | tf_op jit(solution)/shard_map/all_to_all | solution.py:240
  150.6 16.0 %all-to-all-done.3 = bf16[32,96,128]{2,1,0:T(8,128)(2,1)S(1)} async-done(((bf16[32,96,128]{2,1,0:T(8,128)(2,1)}), bf16[32,96,128]{2,1,0:T(8,128)(2,1)S(1)}, u32[]{:S(2)}, u32[]{:S(2)}) %all-to-all-start.3) | async-done | bytes 786464 | tf_op jit(solution)/shard_map/all_to_all | solution.py:240
  166.6 0.7 bitcast_reduce_fusion
  167.3 11.4 %all-to-all-start.4 = ((bf16[16,24,128]{2,1,0:T(8,128)(2,1)}), bf16[16,24,128]{2,1,0:T(8,128)(2,1)S(1)}, u32[]{:S(2)}, u32[]{:S(2)}) async-start(bf16[16,24,128]{2,1,0:T(8,128)(2,1)} %bitcast.21), calls=%async_computation.4 | async-start | bytes 196608 | tf_op jit(solution)/shard_map/all_to_all | solution.py:244
  178.8 9.7 %all-to-all-done.4 = bf16[16,24,128]{2,1,0:T(8,128)(2,1)S(1)} async-done(((bf16[16,24,128]{2,1,0:T(8,128)(2,1)}), bf16[16,24,128]{2,1,0:T(8,128)(2,1)S(1)}, u32[]{:S(2)}, u32[]{:S(2)}) %all-to-all-start.4) | async-done | bytes 98336 | tf_op jit(solution)/shard_map/all_to_all | solution.py:244
  188.8 0.6 fusion.29
  (55 shorter events, 2.5 us)
Async XLA Ops:
  6.5 16.8 %copy-start = (s32[2048,2]{0,1:T(2,128)S(1)}, s32[2048,2]{0,1:T(2,128)}, u32[]{:S(2)}) copy-start(s32[2048,2]{0,1:T(2,128)} %param.15) | copy-start | bytes 49156
  6.5 16.8 %copy-start.4 = (bf16[64,256]{1,0:T(8,128)(2,1)S(1)}, bf16[64,256]{1,0:T(8,128)(2,1)}, u32[]{:S(2)}) copy-start(bf16[64,256]{1,0:T(8,128)(2,1)} %param.10) | copy-start | bytes 98308
  6.5 17.5 %copy-start.6 = (bf16[256]{0:T(256)(128)(2,1)S(1)}, bf16[256]{0:T(256)(128)(2,1)}, u32[]{:S(2)}) copy-start(bf16[256]{0:T(256)(128)(2,1)} %param.14) | copy-start | bytes 1540
  8.2 29.2 %all-to-all-start = ((bf16[32,64,128]{2,1,0:T(8,128)(2,1)}), bf16[32,64,128]{2,1,0:T(8,128)(2,1)S(1)}, u32[]{:S(2)}, u32[]{:S(2)}) async-start(bf16[32,64,128]{2,1,0:T(8,128)(2,1)} %broadcast_in_dim.74), calls=%async_computation | async-start | bytes 1048576 | tf_op jit(solution)/shard_map/all_to_all | solution.py:191
  22.5 54.6 %all-gather.6.cloned.1.call-start = ((), (), s32[]{:S(2)}) async-start(), calls=%async_computation.6 | async-start | bytes 3145728 | tf_op jit(solution)/shard_map/all_gather | solution.py:190
  23.3 96.6 %all-gather.4.cloned.1.call-start = ((), (), s32[]{:S(2)}) async-start(), calls=%async_computation.5 | async-start | bytes 1769472 | tf_op jit(solution)/shard_map/all_gather | solution.py:233
  37.4 6.3 %collective-permute-start = (bf16[2048,128]{1,0:T(8,128)(2,1)S(1)}, bf16[2048,128]{1,0:T(8,128)(2,1)S(1)}, u32[]{:S(2)}, u32[]{:S(2)}) collective-permute-start(bf16[2048,128]{1,0:T(8,128)(2,1)S(1)} %bitcast.56), channel_id=1, source_target_pairs={{0,1},{1,0},{2,3},{3,2},{4,5},{5,4},{6,7},{7,6},{8,9},{9,8},{10,11... | collective-permute-start | bytes 1572872 | tf_op jit(solution)/shard_map/ppermute | solution.py:28
  44.1 0.8 copy-start.3
  45.2 24.2 %copy-start.2 = (bf16[1,4096,128]{2,1,0:T(8,128)(2,1)S(1)}, bf16[1,4096,128]{2,1,0:T(8,128)(2,1)}, u32[]{:S(2)}) copy-start(bf16[1,4096,128]{2,1,0:T(8,128)(2,1)} %param.19) | copy-start | bytes 3145732
  69.4 5.0 %copy-start.1 = (bf16[1,4096,128]{2,1,0:T(8,128)(2,1)S(1)}, bf16[1,4096,128]{2,1,0:T(8,128)(2,1)}, u32[]{:S(2)}) copy-start(bf16[1,4096,128]{2,1,0:T(8,128)(2,1)} %param.18) | copy-start | bytes 3145732
  70.5 37.2 %all-to-all-start.2 = ((bf16[8,512,128]{2,1,0:T(8,128)(2,1)}), bf16[8,512,128]{2,1,0:T(8,128)(2,1)S(1)}, u32[]{:S(2)}, u32[]{:S(2)}) async-start(bf16[8,512,128]{2,1,0:T(8,128)(2,1)} %bitcast.19), calls=%async_computation.2 | async-start | bytes 2097152 | tf_op jit(solution)/shard_map/all_to_all | solution.py:236
  74.4 25.3 %collective-permute-start.2 = (bf16[4096,128]{1,0:T(8,128)(2,1)S(1)}, bf16[4096,128]{1,0:T(8,128)(2,1)}, u32[]{:S(2)}, u32[]{:S(2)}) collective-permute-start(bf16[4096,128]{1,0:T(8,128)(2,1)S(1)} %bitcast.50), channel_id=1, source_target_pairs={{0,128},{128,0},{1,129},{129,1},{2,130},{130,2},{3,131},{131,3},{4... | collective-permute-start | bytes 3145736 | tf_op jit(solution)/shard_map/ppermute | solution.py:28
  77.1 34.0 %collective-permute-start.1 = (bf16[2,4096,128]{2,1,0:T(8,128)(2,1)}, bf16[2,4096,128]{2,1,0:T(8,128)(2,1)}, u32[]{:S(2)}, u32[]{:S(2)}) collective-permute-start(bf16[2,4096,128]{2,1,0:T(8,128)(2,1)} %all-gather.6.cloned.1.call-done.gate_own), channel_id=1, source_target_pairs={{0,1},{1,0},{2,3},{3,2},{4,5},{5,4},{6,7},{7,6},{8,9},{9,8},{10,11... | collective-permute-start | bytes 6291464 | tf_op jit(solution)/shard_map/ppermute | solution.py:28
  81.3 29.8 %collective-permute-start.3 = (bf16[4096,128]{1,0:T(8,128)(2,1)S(1)}, bf16[4096,128]{1,0:T(8,128)(2,1)}, u32[]{:S(2)}, u32[]{:S(2)}) collective-permute-start(bf16[4096,128]{1,0:T(8,128)(2,1)S(1)} %bitcast.51), channel_id=1, source_target_pairs={{0,1},{1,0},{2,3},{3,2},{4,5},{5,4},{6,7},{7,6},{8,9},{9,8},{10,11... | collective-permute-start | bytes 3145736 | tf_op jit(solution)/shard_map/ppermute | solution.py:28
  99.7 11.4 %collective-permute-start.4 = (bf16[4096,128]{1,0:T(8,128)(2,1)}, bf16[4096,128]{1,0:T(8,128)(2,1)}, u32[]{:S(2)}, u32[]{:S(2)}) collective-permute-start(bf16[4096,128]{1,0:T(8,128)(2,1)} %collective-permute-done.2.refs_1_), channel_id=1, source_target_pairs={{0,1},{1,0},{2,3},{3,2},{4,5},{5,4},{6,7},{7,6},{8,9},{9,8},{10,11... | collective-permute-start | bytes 3145736 | tf_op jit(solution)/shard_map/ppermute | solution.py:28
  107.7 34.0 %collective-permute-start.5 = (bf16[8,512,128]{2,1,0:T(8,128)(2,1)S(1)}, bf16[8,512,128]{2,1,0:T(8,128)(2,1)S(1)}, u32[]{:S(2)}, u32[]{:S(2)}) collective-permute-start(bf16[8,512,128]{2,1,0:T(8,128)(2,1)S(1)} %all-to-all-done.2.own), channel_id=1, source_target_pairs={{0,1},{1,0},{2,3},{3,2},{4,5},{5,4},{6,7},{7,6},{8,9},{9,8},{10,11... | collective-permute-start | bytes 3145736 | tf_op jit(solution)/shard_map/ppermute | solution.py:28
  141.7 9.0 %copy-start.5 = (f32[64,2]{0,1:T(2,128)S(1)}, f32[64,2]{0,1:T(2,128)}, u32[]{:S(2)}) copy-start(f32[64,2]{0,1:T(2,128)} %param.16) | copy-start | bytes 1540
  143.7 22.9 %all-to-all-start.3 = ((bf16[32,96,128]{2,1,0:T(8,128)(2,1)}), bf16[32,96,128]{2,1,0:T(8,128)(2,1)S(1)}, u32[]{:S(2)}, u32[]{:S(2)}) async-start(bf16[32,96,128]{2,1,0:T(8,128)(2,1)} %shard_map.101), calls=%async_computation.3 | async-start | bytes 1572864 | tf_op jit(solution)/shard_map/all_to_all | solution.py:240
  167.3 21.2 %all-to-all-start.4 = ((bf16[16,24,128]{2,1,0:T(8,128)(2,1)}), bf16[16,24,128]{2,1,0:T(8,128)(2,1)S(1)}, u32[]{:S(2)}, u32[]{:S(2)}) async-start(bf16[16,24,128]{2,1,0:T(8,128)(2,1)} %bitcast.21), calls=%async_computation.4 | async-start | bytes 196608 | tf_op jit(solution)/shard_map/all_to_all | solution.py:244
Sparse Core Ops, SparseCore 0:
  25.4 45.7 all-gather.5
  73.3 46.4 all-gather.3

commit v4 on v3

--- a/solution.py
+++ b/solution.py
@@ -63,49 +63,53 @@
 
 
 def gate_up_kernel(place, rows, gate_own, gate_far, *refs):
-    uppers, out, total = refs[0:4], refs[4], refs[5]
+    sides, uppers, out, total = (refs[0:2], refs[2:4]), refs[4:8], refs[8], refs[9]
     step = pl.program_id(0)
-    columns = [gate_own[0], gate_own[1], gate_far[0], gate_far[1]] + [ref[...] for ref in uppers]
-    product = jnp.dot(
-        rows[...], jnp.concatenate(columns, axis=1), preferred_element_type=jnp.float32
-    )
+
+    def product(side, side_far):
+        columns = [ref[...] for ref in (gate_own, side, gate_far, side_far, *uppers)]
+        return jnp.dot(
+            rows[...], jnp.concatenate(columns, axis=1), preferred_element_type=jnp.float32
+        )
 
     @pl.when(step == 0)
     def _():
-        total[...] = product
-
-    @pl.when(step != 0)
+        total[...] = product(*sides[0])
+
+    @pl.when(step == 1)
     def _():
-        total[...] += product
-
-    @pl.when(step == pl.num_programs(0) - 1)
-    def _():
-        unit = gate_own.shape[2]
+        total[...] += product(*sides[1])
+        width = out.shape[1]
+        unit = width // 4
         first = place[1] == 0
         for part in range(2):
-            mine = total[:, (4 + 2 * part) * unit : (5 + 2 * part) * unit]
-            side = total[:, (5 + 2 * part) * unit : (6 + 2 * part) * unit]
+            pair = []
             for half in range(2):
-                at = 2 * part + half
-                gate = total[:, at * unit : (at + 1) * unit]
-                upper = jnp.where(first, mine, side) if half == 0 else jnp.where(first, side, mine)
-                hidden = gate / (1.0 + jnp.exp(-gate)) * upper
-                out[:, at * unit : (at + 1) * unit] = hidden.astype(jnp.bfloat16)
-
-
-def gate_up(place, rows, gates, uppers):
+                at = (2 * part + half) * unit
+                gate = total[:, at : at + unit]
+                upper = total[:, width + at : width + at + unit]
+                pair.append((gate / (1.0 + jnp.exp(-gate)) * upper).astype(jnp.bfloat16))
+            at = 2 * part * unit
+            out[:, at : at + unit] = jnp.where(first, pair[0], pair[1])
+            out[:, at + unit : at + 2 * unit] = jnp.where(first, pair[1], pair[0])
+
+
+def gate_up(place, rows, gates, sides, uppers):
     count, depth = rows.shape
     unit = uppers[0].shape[1]
-    chunk = 2048
+    chunk = depth // 2
+    by_step = pl.BlockSpec((chunk, unit), lambda i, place: (i, 0))
+    fixed = pl.BlockSpec((chunk, unit), lambda i, place: (0, 0))
     return pl.pallas_call(
         gate_up_kernel,
         out_shape=jax.ShapeDtypeStruct((count, 4 * unit), jnp.bfloat16),
         grid_spec=pltpu.PrefetchScalarGridSpec(
             num_scalar_prefetch=1,
-            grid=(depth // chunk,),
+            grid=(2,),
             in_specs=[pl.BlockSpec((count, chunk), lambda i, place: (0, i))]
-            + [pl.BlockSpec((2, chunk, unit), lambda i, place: (0, i, 0))] * 2
-            + [pl.BlockSpec((chunk, unit), lambda i, place: (i, 0))] * 4,
+            + [by_step] * 2
+            + [fixed] * 4
+            + [by_step] * 4,
             out_specs=pl.BlockSpec((count, 4 * unit), lambda i, place: (0, 0)),
             scratch_shapes=[pltpu.VMEM((count, 8 * unit), jnp.float32)],
         ),
@@ -115,7 +119,7 @@
             bytes_accessed=2 * depth * (count + 8 * unit),
             transcendentals=count * 4 * unit,
         ),
-    )(place, rows, *gates, *uppers)
+    )(place, rows, *gates, *sides, *uppers)
 
 
 def down_kernel(hidden, own, far, out, product, sorted_rows):
@@ -187,11 +191,14 @@
     key_part = lax.dynamic_slice_in_dim(keys, head, HEAD_DIM, 1)
     value_part = lax.dynamic_slice_in_dim(values, head, HEAD_DIM, 1)
     sent = jnp.where(core == 0, key_part, value_part)
-    gate_own = lax.all_gather(w_gate[0], "ya")
+    middle = w_gate.shape[1] // 2
     held = lax.all_to_all(
         jnp.broadcast_to(sent[None], (ctx_count, seq_rows, HEAD_DIM)), CTX, 0, 0, tiled=True
     ).reshape(ctx_count * seq_rows, HEAD_DIM)
-    w_up, w_down, held = lax.optimization_barrier((w_up, w_down, held))
+    low_own, high_own = w_gate[0, :middle], w_gate[0, middle:]
+    w_up, w_down, held, low_own, high_own = lax.optimization_barrier(
+        (w_up, w_down, held, low_own, high_own)
+    )
     up_side = swap(w_up[0], "ya")
     far = swap(held, "k")
     all_keys = jnp.where(core == 0, held, far)
@@ -217,10 +224,13 @@
         [stream, gain[None, :], jnp.zeros((15, width), jnp.bfloat16)], axis=0
     )
     outgoing = jnp.dot(table, source, preferred_element_type=jnp.float32).astype(jnp.bfloat16)
+    low_side = swap(low_own, "ya")
     outgoing = jnp.broadcast_to(
         outgoing.reshape(1, exp_count, PAD, width), (2, exp_count, PAD, width)
     ).reshape(2 * exp_count, PAD, width)
     arrived = lax.all_to_all(outgoing, ("yp",) + EXP, 0, 0, tiled=True)
+    arrived, low_side, cut = lax.optimization_barrier((arrived, low_side, cut))
+    high_side = swap(high_own, "ya")
     arrived = arrived.reshape(2, exp_count, PAD, width).astype(jnp.float32)
     rows = arrived[:, :, :HALF]
     all_gain = arrived[0, :, HALF]
@@ -230,12 +240,21 @@
     )
     piece = jnp.transpose(normed, (0, 2, 1, 3)).reshape(CAP, exp_count * width)
 
-    all_rows = lax.all_gather(piece, "z", axis=0, tiled=True)
-    gates = [gate_own, swap(gate_own, "k")]
-    uppers = [w_up[0], up_side, swap(w_up[0], "k"), swap(up_side, "k")]
+    all_rows = lax.all_to_all(
+        jnp.broadcast_to(piece[None], (z_count,) + piece.shape), "z", 0, 0, tiled=True
+    ).reshape(z_count * CAP, piece.shape[1])
+    gate_far, up_far, low_side_far = swap(w_gate[0], "k"), swap(w_up[0], "k"), swap(low_side, "k")
+    high_side, up_side, gate_far, up_far, low_side_far = lax.optimization_barrier(
+        (high_side, up_side, gate_far, up_far, low_side_far)
+    )
+    gates = [w_gate[0], gate_far]
+    sides = [low_side, low_side_far, high_side, swap(high_side, "k")]
+    uppers = [w_up[0], up_side, up_far, swap(up_side, "k")]
+    all_rows, cut = lax.optimization_barrier((all_rows, cut))
     down_own = lax.all_to_all(cut, "z", 0, 0, tiled=True)
-    hidden = gate_up(place, all_rows, gates, uppers)
+    hidden = gate_up(place, all_rows, gates, sides, uppers)
     hidden = lax.all_gather(hidden, ("yp", "ya"))
+    hidden, down_own = lax.optimization_barrier((hidden, down_own))
     back = down(hidden, down_own, swap(down_own, "k"), ctx_count)
     back = lax.all_to_all(back, CTX, 0, 0, tiled=True)
     back = back.reshape(ctx_count // z_count, z_count, z_count * HALF, unit).astype(jnp.float32)

time: 197 us -> 198 us (level)
  blocking collectives: 38.4 us -> 16.6 us
  starting transfers between devices: 57 us -> 75.7 us
  between operations: 13.7 us -> 0.41 us
  waiting for transfers between devices: 69.7 us -> 81.9 us
  local copies, waits for them, and re-layouts: 3.97 us -> 8.43 us
    all_to_all x0 -> x2, waiting for transfers between devices: none -> 34.7 us  [the longest x1 24.7 us: shards(): lax.all_to_all(jnp.broadcast_to(piece[None], (z_count,) + piece.shape), '...]
    all_to_all x1 -> x0, blocking collectives: 22.9 us -> none  [shards(): arrived = lax.all_to_all(outgoing, ('yp',) + EXP, 0, 0, tiled=True)]
    ppermute x6 -> x10, waiting for transfers between devices: 17.7 us -> 5.19 us  [swap(): return lax.ppermute(value, axis, SWAP)]
    ppermute x6 -> x10, starting transfers between devices: 20.6 us -> 31.9 us  [swap(): return lax.ppermute(value, axis, SWAP)]
    all_to_all x0 -> x2, starting transfers between devices: none -> 10.9 us  [the longest x1 7.31 us: shards(): arrived = lax.all_to_all(outgoing, ('yp',) + EXP, 0, 0, tiled=True)]
    all_gather x2 -> x0, waiting for transfers between devices: 8.71 us -> none  [the longest x1 8.69 us: shards(): all_rows = lax.all_gather(piece, 'z', axis=0, tiled=True)]
    all_to_all x1, starting transfers between devices: 11.4 us -> 6.38 us  [shards(): lax.all_to_all(summed.reshape(exp_count, tall, unit), EXP, 0, 0, tiled=True)]
    all_to_all x1, waiting for transfers between devices: 16 us -> 20.4 us  [shards(): back = lax.all_to_all(back, CTX, 0, 0, tiled=True)]
  transfers between devices with their start and end apart: 12 -> 16, of which waited for: 7 -> 8; matrix products, arithmetic and copies ran while one was open for 3% -> 4% of each run, Pallas kernels for 3% -> 3%
where the time goes in v4:
time: 198 us; the launch traced here: 197 us
  waiting for transfers between devices  81.9 us (41%)
  starting transfers between devices  75.7 us (38%)
  blocking collectives  16.6 us (8%)
  Pallas kernels  8.62 us (4%)
  local copies, waits for them, and re-layouts  8.43 us (4%)
  other arithmetic  3.59 us (2%)
    ppermute x10, starting transfers between devices, swap(): return lax.ppermute(value, axis, SWAP)  31.9 us
    all_to_all x1, waiting for transfers between devices, shards(): lax.all_to_all(jnp.broadcast_to(piece[None], (z_count,) + piece.shape), '...  24.7 us
    all_to_all x1, waiting for transfers between devices, shards(): back = lax.all_to_all(back, CTX, 0, 0, tiled=True)  20.4 us
    all_gather x1, blocking collectives, shards(): hidden = lax.all_gather(hidden, ('yp', 'ya'))  16.6 us
    all_to_all x1, starting transfers between devices, shards(): lax.all_to_all(jnp.broadcast_to(sent[None], (ctx_count, seq_rows, HEAD_DI...  14.3 us
    all_to_all x1, waiting for transfers between devices, shards(): lax.all_to_all(jnp.broadcast_to(sent[None], (ctx_count, seq_rows, HEAD_DI...  11.9 us
    all_to_all x1, waiting for transfers between devices, shards(): arrived = lax.all_to_all(outgoing, ('yp',) + EXP, 0, 0, tiled=True)  10 us
    all_to_all x1, waiting for transfers between devices, shards(): lax.all_to_all(summed.reshape(exp_count, tall, unit), EXP, 0, 0, tiled=True)  9.63 us
  transfers between devices with their start and end apart: 16, of which 8 were waited for; matrix products, arithmetic and copies ran while one was open for 4% of the time, Pallas kernels for 3%

profile of v4, /device:TPU:1, one launch (start us, length us, event | category | flops | bytes accessed | tf_op | source)
XLA Modules:
  0.0 196.7 jit_solution(9494224762622870758)
XLA Ops:
  0.8 0.9 broadcast_in_dim.81
  1.7 14.3 %all-to-all-start = ((bf16[32,64,128]{2,1,0:T(8,128)(2,1)}), bf16[32,64,128]{2,1,0:T(8,128)(2,1)S(1)}, u32[]{:S(2)}, u32[]{:S(2)}) async-start(bf16[32,64,128]{2,1,0:T(8,128)(2,1)} %broadcast_in_dim.81), calls=%async_computation | async-start | bytes 1048576 | tf_op jit(solution)/shard_map/all_to_all | solution.py:195
  16.9 2.1 %slice_bitcast_fusion = (bf16[2048,128]{1,0:T(8,128)(2,1)}, bf16[2048,128]{1,0:T(8,128)(2,1)S(1)}) fusion(bf16[1,4096,128]{2,1,0:T(8,128)(2,1)} %param.17), kind=kLoop, calls=%fused_computation.19 | loop fusion | bytes 2097152 | tf_op jit(solution)/shard_map/squeeze | solution.py:198
  19.0 11.9 %all-to-all-done = bf16[32,64,128]{2,1,0:T(8,128)(2,1)S(1)} async-done(((bf16[32,64,128]{2,1,0:T(8,128)(2,1)}), bf16[32,64,128]{2,1,0:T(8,128)(2,1)S(1)}, u32[]{:S(2)}, u32[]{:S(2)}) %all-to-all-start) | async-done | bytes 524320 | tf_op jit(solution)/shard_map/all_to_all | solution.py:195
  30.9 4.8 %collective-permute-start = (bf16[2048,128]{1,0:T(8,128)(2,1)S(1)}, bf16[2048,128]{1,0:T(8,128)(2,1)S(1)}, u32[]{:S(2)}, u32[]{:S(2)}) collective-permute-start(bf16[2048,128]{1,0:T(8,128)(2,1)S(1)} %bitcast.60), channel_id=1, source_target_pairs={{0,1},{1,0},{2,3},{3,2},{4,5},{5,4},{6,7},{7,6},{8,9},{9,8},{10,11... | collective-permute-start | bytes 1572872 | tf_op jit(solution)/shard_map/ppermute | solution.py:28
  36.0 3.2 %collective-permute-start.1 = (bf16[2048,128]{1,0:T(8,128)(2,1)S(1)}, bf16[2048,128]{1,0:T(8,128)(2,1)S(1)}, u32[]{:S(2)}, u32[]{:S(2)}) collective-permute-start(bf16[2048,128]{1,0:T(8,128)(2,1)S(1)} %get-tuple-element.23), channel_id=1, source_target_pairs={{0,128},{128,0},{1,129},{129,1},{2,130},{130,2},{3,131},{131,3},{4... | collective-permute-start | bytes 1572872 | tf_op jit(solution)/shard_map/ppermute | solution.py:28
  41.6 7.3 %all-to-all-start.1 = ((bf16[32,16,256]{2,1,0:T(8,128)(2,1)}), bf16[32,16,256]{2,1,0:T(8,128)(2,1)S(1)}, u32[]{:S(2)}, u32[]{:S(2)}) async-start(bf16[32,16,256]{2,1,0:T(8,128)(2,1)} %bitcast.13), calls=%async_computation.1 | async-start | bytes 524288 | tf_op jit(solution)/shard_map/all_to_all | solution.py:231
  49.0 1.1 copy.20
  50.0 1.4 collective-permute-done.1.refs_0_
  51.4 10.0 %all-to-all-done.1 = bf16[32,16,256]{2,1,0:T(8,128)(2,1)S(1)} async-done(((bf16[32,16,256]{2,1,0:T(8,128)(2,1)}), bf16[32,16,256]{2,1,0:T(8,128)(2,1)S(1)}, u32[]{:S(2)}, u32[]{:S(2)}) %all-to-all-start.1) | async-done | bytes 262176 | tf_op jit(solution)/shard_map/all_to_all | solution.py:231
  61.9 1.3 broadcast_in_dim.95
  63.3 3.6 %all-to-all-start.2 = ((bf16[8,24,4096]{2,1,0:T(8,128)(2,1)}), bf16[8,24,4096]{2,1,0:T(8,128)(2,1)S(1)}, u32[]{:S(2)}, u32[]{:S(2)}) async-start(bf16[8,24,4096]{2,1,0:T(8,128)(2,1)} %broadcast_in_dim.95), calls=%async_computation.2 | async-start | bytes 3145728 | tf_op jit(solution)/shard_map/all_to_all | solution.py:243
  66.9 3.4 %collective-permute-start.4 = (bf16[4096,128]{1,0:T(8,128)(2,1)}, bf16[4096,128]{1,0:T(8,128)(2,1)}, u32[]{:S(2)}, u32[]{:S(2)}) collective-permute-start(bf16[4096,128]{1,0:T(8,128)(2,1)} %bitcast.21.gate_own), channel_id=1, source_target_pairs={{0,1},{1,0},{2,3},{3,2},{4,5},{5,4},{6,7},{7,6},{8,9},{9,8},{10,11... | collective-permute-start | bytes 3145736 | tf_op jit(solution)/shard_map/ppermute | solution.py:28
  70.3 2.9 %collective-permute-start.3 = (bf16[4096,128]{1,0:T(8,128)(2,1)}, bf16[4096,128]{1,0:T(8,128)(2,1)}, u32[]{:S(2)}, u32[]{:S(2)}) collective-permute-start(bf16[4096,128]{1,0:T(8,128)(2,1)} %bitcast.22.refs_4_), channel_id=1, source_target_pairs={{0,128},{128,0},{1,129},{129,1},{2,130},{130,2},{3,131},{131,3},{4... | collective-permute-start | bytes 3145736 | tf_op jit(solution)/shard_map/ppermute | solution.py:28
  73.2 2.2 %collective-permute-start.5 = (bf16[4096,128]{1,0:T(8,128)(2,1)}, bf16[4096,128]{1,0:T(8,128)(2,1)}, u32[]{:S(2)}, u32[]{:S(2)}) collective-permute-start(bf16[4096,128]{1,0:T(8,128)(2,1)} %bitcast.22.refs_4_), channel_id=1, source_target_pairs={{0,1},{1,0},{2,3},{3,2},{4,5},{5,4},{6,7},{7,6},{8,9},{9,8},{10,11... | collective-permute-start | bytes 3145736 | tf_op jit(solution)/shard_map/ppermute | solution.py:28
  75.4 2.4 %collective-permute-start.2 = (bf16[2048,128]{1,0:T(8,128)(2,1)}, bf16[2048,128]{1,0:T(8,128)(2,1)}, u32[]{:S(2)}, u32[]{:S(2)}) collective-permute-start(bf16[2048,128]{1,0:T(8,128)(2,1)} %get-tuple-element.28), channel_id=1, source_target_pairs={{0,128},{128,0},{1,129},{129,1},{2,130},{130,2},{3,131},{131,3},{4... | collective-permute-start | bytes 1572872 | tf_op jit(solution)/shard_map/ppermute | solution.py:28
  77.8 2.4 %collective-permute-start.6 = (bf16[2048,128]{1,0:T(8,128)(2,1)S(1)}, bf16[2048,128]{1,0:T(8,128)(2,1)}, u32[]{:S(2)}, u32[]{:S(2)}) collective-permute-start(bf16[2048,128]{1,0:T(8,128)(2,1)S(1)} %collective-permute-done.1.refs_0_), channel_id=1, source_target_pairs={{0,1},{1,0},{2,3},{3,2},{4,5},{5,4},{6,7},{7,6},{8,9},{9,8},{10,11... | collective-permute-start | bytes 1572872 | tf_op jit(solution)/shard_map/ppermute | solution.py:28
  80.2 24.7 %all-to-all-done.2 = bf16[8,24,4096]{2,1,0:T(8,128)(2,1)S(1)} async-done(((bf16[8,24,4096]{2,1,0:T(8,128)(2,1)}), bf16[8,24,4096]{2,1,0:T(8,128)(2,1)S(1)}, u32[]{:S(2)}, u32[]{:S(2)}) %all-to-all-start.2) | async-done | bytes 1572896 | tf_op jit(solution)/shard_map/all_to_all | solution.py:243
  104.9 3.7 %all-to-all-start.3 = ((bf16[8,512,128]{2,1,0:T(8,128)(2,1)}), bf16[8,512,128]{2,1,0:T(8,128)(2,1)S(1)}, u32[]{:S(2)}, u32[]{:S(2)}) async-start(bf16[8,512,128]{2,1,0:T(8,128)(2,1)} %bitcast.56), calls=%async_computation.3 | async-start | bytes 2097152 | tf_op jit(solution)/shard_map/all_to_all | solution.py:254
  108.6 4.7 %collective-permute-start.8 = (bf16[4096,128]{1,0:T(8,128)(2,1)}, bf16[4096,128]{1,0:T(8,128)(2,1)}, u32[]{:S(2)}, u32[]{:S(2)}) collective-permute-start(bf16[4096,128]{1,0:T(8,128)(2,1)} %collective-permute-done.3.refs_5_), channel_id=1, source_target_pairs={{0,1},{1,0},{2,3},{3,2},{4,5},{5,4},{6,7},{7,6},{8,9},{9,8},{10,11... | collective-permute-start | bytes 3145736 | tf_op jit(solution)/shard_map/ppermute | solution.py:28
  113.3 1.9 collective-permute-start.7
  115.8 1.5 collective-permute-done.7.refs_3_
  117.3 0.8 copy-done.4
  118.1 6.6 %shard_map.100 = bf16[192,512]{1,0:T(8,128)(2,1)} custom-call(s32[2]{0:T(128)} %pad_add_fusion.place, bf16[192,4096]{1,0:T(8,128)(2,1)} %bitcast.55, bf16[4096,128]{1,0:T(8,128)(2,1)} %bitcast.21.gate_own, bf16[4096,128]{1,0:T(8,128)(2,1)} %collective-permute-done.4.gate_far, bf16[2048,128]{1,0:T(8,128)(2,1)} %copy-done.3, ...), custom_call_target="tpu_custom_call" | custom-call | flops 1610612736 | bytes 9961472 | tf_op jit(solution)/shard_map/pallas_call | solution.py:103
  124.7 16.6 %all-gather = bf16[768,512]{1,0:T(8,128)(2,1)S(1)} all-gather(bf16[192,512]{1,0:T(8,128)(2,1)} %shard_map.100), channel_id=2, replica_groups=mesh['yp'=2,'ya'=2,'z'=8,'x'=4,'h'=2,'k'=2] {'yp','ya'}, dimensions={0}, use_global_device_ids=true | all-gather | bytes 983040 | tf_op jit(solution)/shard_map/all_gather | solution.py:256
  141.4 4.1 %collective-permute-start.9 = (bf16[8,512,128]{2,1,0:T(8,128)(2,1)S(1)}, bf16[8,512,128]{2,1,0:T(8,128)(2,1)S(1)}, u32[]{:S(2)}, u32[]{:S(2)}) collective-permute-start(bf16[8,512,128]{2,1,0:T(8,128)(2,1)S(1)} %all-to-all-done.3.own), channel_id=1, source_target_pairs={{0,1},{1,0},{2,3},{3,2},{4,5},{5,4},{6,7},{7,6},{8,9},{9,8},{10,11... | collective-permute-start | bytes 3145736 | tf_op jit(solution)/shard_map/ppermute | solution.py:28
  145.4 2.3 %collective-permute-done.9.far = bf16[8,512,128]{2,1,0:T(8,128)(2,1)S(1)} collective-permute-done((bf16[8,512,128]{2,1,0:T(8,128)(2,1)S(1)}, bf16[8,512,128]{2,1,0:T(8,128)(2,1)S(1)}, u32[]{:S(2)}, u32[]{:S(2)}) %collective-permute-start.9) | collective-permute-done | bytes 1048608 | tf_op jit(solution)/shard_map/ppermute | solution.py:28
  147.7 2.0 %shard_map.101 = bf16[32,96,128]{2,1,0:T(8,128)(2,1)} custom-call(bf16[4,192,512]{2,1,0:T(8,128)(2,1)S(1)} %bitcast.54, bf16[8,512,128]{2,1,0:T(8,128)(2,1)S(1)} %all-to-all-done.3.own, bf16[8,512,128]{2,1,0:T(8,128)(2,1)S(1)} %collective-permute-done.9.far), custom_call_target="tpu_custom_call" | custom-call | flops 805306368 | bytes 3670016 | tf_op jit(solution)/shard_map/pallas_call | solution.py:161
  149.7 8.6 %all-to-all-start.4 = ((bf16[32,96,128]{2,1,0:T(8,128)(2,1)}), bf16[32,96,128]{2,1,0:T(8,128)(2,1)S(1)}, u32[]{:S(2)}, u32[]{:S(2)}) async-start(bf16[32,96,128]{2,1,0:T(8,128)(2,1)} %shard_map.101), calls=%async_computation.4 | async-start | bytes 1572864 | tf_op jit(solution)/shard_map/all_to_all | solution.py:259
  158.6 20.4 %all-to-all-done.4 = bf16[32,96,128]{2,1,0:T(8,128)(2,1)S(1)} async-done(((bf16[32,96,128]{2,1,0:T(8,128)(2,1)}), bf16[32,96,128]{2,1,0:T(8,128)(2,1)S(1)}, u32[]{:S(2)}, u32[]{:S(2)}) %all-to-all-start.4) | async-done | bytes 786464 | tf_op jit(solution)/shard_map/all_to_all | solution.py:259
  179.7 6.4 %all-to-all-start.5 = ((bf16[16,24,128]{2,1,0:T(8,128)(2,1)}), bf16[16,24,128]{2,1,0:T(8,128)(2,1)S(1)}, u32[]{:S(2)}, u32[]{:S(2)}) async-start(bf16[16,24,128]{2,1,0:T(8,128)(2,1)} %bitcast.25), calls=%async_computation.5 | async-start | bytes 196608 | tf_op jit(solution)/shard_map/all_to_all | solution.py:263
  186.2 9.6 %all-to-all-done.5 = bf16[16,24,128]{2,1,0:T(8,128)(2,1)S(1)} async-done(((bf16[16,24,128]{2,1,0:T(8,128)(2,1)}), bf16[16,24,128]{2,1,0:T(8,128)(2,1)S(1)}, u32[]{:S(2)}, u32[]{:S(2)}) %all-to-all-start.5) | async-done | bytes 98336 | tf_op jit(solution)/shard_map/all_to_all | solution.py:263
  (66 shorter events, 7.3 us)
Async XLA Ops:
  0.0 16.0 %copy-start = (s32[2048,2]{0,1:T(2,128)S(1)}, s32[2048,2]{0,1:T(2,128)}, u32[]{:S(2)}) copy-start(s32[2048,2]{0,1:T(2,128)} %param.15) | copy-start | bytes 49156
  0.0 16.7 %copy-start.8 = (bf16[256]{0:T(256)(128)(2,1)S(1)}, bf16[256]{0:T(256)(128)(2,1)}, u32[]{:S(2)}) copy-start(bf16[256]{0:T(256)(128)(2,1)} %param.14) | copy-start | bytes 1540
  0.0 16.8 %copy-start.6 = (bf16[64,256]{1,0:T(8,128)(2,1)S(1)}, bf16[64,256]{1,0:T(8,128)(2,1)}, u32[]{:S(2)}) copy-start(bf16[64,256]{1,0:T(8,128)(2,1)} %param.10) | copy-start | bytes 98308
  1.7 29.2 %all-to-all-start = ((bf16[32,64,128]{2,1,0:T(8,128)(2,1)}), bf16[32,64,128]{2,1,0:T(8,128)(2,1)S(1)}, u32[]{:S(2)}, u32[]{:S(2)}) async-start(bf16[32,64,128]{2,1,0:T(8,128)(2,1)} %broadcast_in_dim.81), calls=%async_computation | async-start | bytes 1048576 | tf_op jit(solution)/shard_map/all_to_all | solution.py:195
  30.9 8.3 %collective-permute-start = (bf16[2048,128]{1,0:T(8,128)(2,1)S(1)}, bf16[2048,128]{1,0:T(8,128)(2,1)S(1)}, u32[]{:S(2)}, u32[]{:S(2)}) collective-permute-start(bf16[2048,128]{1,0:T(8,128)(2,1)S(1)} %bitcast.60), channel_id=1, source_target_pairs={{0,1},{1,0},{2,3},{3,2},{4,5},{5,4},{6,7},{7,6},{8,9},{9,8},{10,11... | collective-permute-start | bytes 1572872 | tf_op jit(solution)/shard_map/ppermute | solution.py:28
  36.0 15.4 %collective-permute-start.1 = (bf16[2048,128]{1,0:T(8,128)(2,1)S(1)}, bf16[2048,128]{1,0:T(8,128)(2,1)S(1)}, u32[]{:S(2)}, u32[]{:S(2)}) collective-permute-start(bf16[2048,128]{1,0:T(8,128)(2,1)S(1)} %get-tuple-element.23), channel_id=1, source_target_pairs={{0,128},{128,0},{1,129},{129,1},{2,130},{130,2},{3,131},{131,3},{4... | collective-permute-start | bytes 1572872 | tf_op jit(solution)/shard_map/ppermute | solution.py:28
  39.9 0.8 copy-start.5
  39.9 9.0 %copy-start.2 = (bf16[1,4096,128]{2,1,0:T(8,128)(2,1)S(1)}, bf16[1,4096,128]{2,1,0:T(8,128)(2,1)}, u32[]{:S(2)}) copy-start(bf16[1,4096,128]{2,1,0:T(8,128)(2,1)} %param.19) | copy-start | bytes 3145732
  41.6 19.8 %all-to-all-start.1 = ((bf16[32,16,256]{2,1,0:T(8,128)(2,1)}), bf16[32,16,256]{2,1,0:T(8,128)(2,1)S(1)}, u32[]{:S(2)}, u32[]{:S(2)}) async-start(bf16[32,16,256]{2,1,0:T(8,128)(2,1)} %bitcast.13), calls=%async_computation.1 | async-start | bytes 524288 | tf_op jit(solution)/shard_map/all_to_all | solution.py:231
  51.4 26.3 %copy-start.3 = (bf16[2048,128]{1,0:T(8,128)(2,1)}, bf16[2048,128]{1,0:T(8,128)(2,1)S(1)}, u32[]{:S(2)}) copy-start(bf16[2048,128]{1,0:T(8,128)(2,1)S(1)} %collective-permute-done.1.refs_0_) | copy-start | bytes 1572868
  63.3 41.6 %all-to-all-start.2 = ((bf16[8,24,4096]{2,1,0:T(8,128)(2,1)}), bf16[8,24,4096]{2,1,0:T(8,128)(2,1)S(1)}, u32[]{:S(2)}, u32[]{:S(2)}) async-start(bf16[8,24,4096]{2,1,0:T(8,128)(2,1)} %broadcast_in_dim.95), calls=%async_computation.2 | async-start | bytes 3145728 | tf_op jit(solution)/shard_map/all_to_all | solution.py:243
  66.9 41.7 %collective-permute-start.4 = (bf16[4096,128]{1,0:T(8,128)(2,1)}, bf16[4096,128]{1,0:T(8,128)(2,1)}, u32[]{:S(2)}, u32[]{:S(2)}) collective-permute-start(bf16[4096,128]{1,0:T(8,128)(2,1)} %bitcast.21.gate_own), channel_id=1, source_target_pairs={{0,1},{1,0},{2,3},{3,2},{4,5},{5,4},{6,7},{7,6},{8,9},{9,8},{10,11... | collective-permute-start | bytes 3145736 | tf_op jit(solution)/shard_map/ppermute | solution.py:28
  70.3 38.3 %collective-permute-start.3 = (bf16[4096,128]{1,0:T(8,128)(2,1)}, bf16[4096,128]{1,0:T(8,128)(2,1)}, u32[]{:S(2)}, u32[]{:S(2)}) collective-permute-start(bf16[4096,128]{1,0:T(8,128)(2,1)} %bitcast.22.refs_4_), channel_id=1, source_target_pairs={{0,128},{128,0},{1,129},{129,1},{2,130},{130,2},{3,131},{131,3},{4... | collective-permute-start | bytes 3145736 | tf_op jit(solution)/shard_map/ppermute | solution.py:28
  73.2 35.4 %collective-permute-start.5 = (bf16[4096,128]{1,0:T(8,128)(2,1)}, bf16[4096,128]{1,0:T(8,128)(2,1)}, u32[]{:S(2)}, u32[]{:S(2)}) collective-permute-start(bf16[4096,128]{1,0:T(8,128)(2,1)} %bitcast.22.refs_4_), channel_id=1, source_target_pairs={{0,1},{1,0},{2,3},{3,2},{4,5},{5,4},{6,7},{7,6},{8,9},{9,8},{10,11... | collective-permute-start | bytes 3145736 | tf_op jit(solution)/shard_map/ppermute | solution.py:28
  75.4 33.2 %collective-permute-start.2 = (bf16[2048,128]{1,0:T(8,128)(2,1)}, bf16[2048,128]{1,0:T(8,128)(2,1)}, u32[]{:S(2)}, u32[]{:S(2)}) collective-permute-start(bf16[2048,128]{1,0:T(8,128)(2,1)} %get-tuple-element.28), channel_id=1, source_target_pairs={{0,128},{128,0},{1,129},{129,1},{2,130},{130,2},{3,131},{131,3},{4... | collective-permute-start | bytes 1572872 | tf_op jit(solution)/shard_map/ppermute | solution.py:28
  77.8 30.8 %collective-permute-start.6 = (bf16[2048,128]{1,0:T(8,128)(2,1)S(1)}, bf16[2048,128]{1,0:T(8,128)(2,1)}, u32[]{:S(2)}, u32[]{:S(2)}) collective-permute-start(bf16[2048,128]{1,0:T(8,128)(2,1)S(1)} %collective-permute-done.1.refs_0_), channel_id=1, source_target_pairs={{0,1},{1,0},{2,3},{3,2},{4,5},{5,4},{6,7},{7,6},{8,9},{9,8},{10,11... | collective-permute-start | bytes 1572872 | tf_op jit(solution)/shard_map/ppermute | solution.py:28
  104.9 12.4 %copy-start.1 = (bf16[8,24,4096]{2,1,0:T(8,128)(2,1)}, bf16[8,24,4096]{2,1,0:T(8,128)(2,1)S(1)}, u32[]{:S(2)}) copy-start(bf16[8,24,4096]{2,1,0:T(8,128)(2,1)S(1)} %all-to-all-done.2) | copy-start | bytes 4718596
  104.9 36.4 %all-to-all-start.3 = ((bf16[8,512,128]{2,1,0:T(8,128)(2,1)}), bf16[8,512,128]{2,1,0:T(8,128)(2,1)S(1)}, u32[]{:S(2)}, u32[]{:S(2)}) async-start(bf16[8,512,128]{2,1,0:T(8,128)(2,1)} %bitcast.56), calls=%async_computation.3 | async-start | bytes 2097152 | tf_op jit(solution)/shard_map/all_to_all | solution.py:254
  108.6 8.7 %collective-permute-start.8 = (bf16[4096,128]{1,0:T(8,128)(2,1)}, bf16[4096,128]{1,0:T(8,128)(2,1)}, u32[]{:S(2)}, u32[]{:S(2)}) collective-permute-start(bf16[4096,128]{1,0:T(8,128)(2,1)} %collective-permute-done.3.refs_5_), channel_id=1, source_target_pairs={{0,1},{1,0},{2,3},{3,2},{4,5},{5,4},{6,7},{7,6},{8,9},{9,8},{10,11... | collective-permute-start | bytes 3145736 | tf_op jit(solution)/shard_map/ppermute | solution.py:28
  113.3 4.0 %collective-permute-start.7 = (bf16[2048,128]{1,0:T(8,128)(2,1)}, bf16[2048,128]{1,0:T(8,128)(2,1)S(1)}, u32[]{:S(2)}, u32[]{:S(2)}) collective-permute-start(bf16[2048,128]{1,0:T(8,128)(2,1)} %collective-permute-done.2.refs_2_), channel_id=1, source_target_pairs={{0,1},{1,0},{2,3},{3,2},{4,5},{5,4},{6,7},{7,6},{8,9},{9,8},{10,11... | collective-permute-start | bytes 1572872 | tf_op jit(solution)/shard_map/ppermute | solution.py:28
  117.3 0.8 copy-start.4
  141.4 6.4 %collective-permute-start.9 = (bf16[8,512,128]{2,1,0:T(8,128)(2,1)S(1)}, bf16[8,512,128]{2,1,0:T(8,128)(2,1)S(1)}, u32[]{:S(2)}, u32[]{:S(2)}) collective-permute-start(bf16[8,512,128]{2,1,0:T(8,128)(2,1)S(1)} %all-to-all-done.3.own), channel_id=1, source_target_pairs={{0,1},{1,0},{2,3},{3,2},{4,5},{5,4},{6,7},{7,6},{8,9},{9,8},{10,11... | collective-permute-start | bytes 3145736 | tf_op jit(solution)/shard_map/ppermute | solution.py:28
  149.7 8.8 %copy-start.7 = (f32[64,2]{0,1:T(2,128)S(1)}, f32[64,2]{0,1:T(2,128)}, u32[]{:S(2)}) copy-start(f32[64,2]{0,1:T(2,128)} %param.16) | copy-start | bytes 1540
  149.7 29.2 %all-to-all-start.4 = ((bf16[32,96,128]{2,1,0:T(8,128)(2,1)}), bf16[32,96,128]{2,1,0:T(8,128)(2,1)S(1)}, u32[]{:S(2)}, u32[]{:S(2)}) async-start(bf16[32,96,128]{2,1,0:T(8,128)(2,1)} %shard_map.101), calls=%async_computation.4 | async-start | bytes 1572864 | tf_op jit(solution)/shard_map/all_to_all | solution.py:259
  179.7 16.1 %all-to-all-start.5 = ((bf16[16,24,128]{2,1,0:T(8,128)(2,1)}), bf16[16,24,128]{2,1,0:T(8,128)(2,1)S(1)}, u32[]{:S(2)}, u32[]{:S(2)}) async-start(bf16[16,24,128]{2,1,0:T(8,128)(2,1)} %bitcast.25), calls=%async_computation.5 | async-start | bytes 196608 | tf_op jit(solution)/shard_map/all_to_all | solution.py:263
